TPU v7x, 32 devices: a whole 2x2x4 slice. The times are simulated.
32 devices in a mesh: items: 16 (over z, x, core), blk: 2 (over y).
Axes of the slice: x: 2, y: 2, z: 4, core: 2. Of those that a mesh axis runs over, the one named last changes fastest.
Arguments:
- byte_ids: int32 [32, 2048], P('items', 'blk'), may hold values from 0 to 261
- span_start: int32 [32, 8], P('items'), may hold values from 0 to 1920, as said below
- span_len: int32 [32, 8], P('items'), may hold values from 13 to 128, as said below
- embedding: bfloat16 [262, 768], replicated, may hold values from -6 to 6
- position: bfloat16 [2048, 768], replicated, may hold values from -5 to 5
- mask_vector: bfloat16 [768], replicated, may hold values from -6 to 6
- gain_bytes: bfloat16 [768], replicated, may hold values from 0.5 to 1.5
- key_enc: bfloat16 [768, 256], replicated, may hold values from -0.21875 to 0.21875
- value_enc: bfloat16 [768, 1280], replicated, may hold values from -0.21875 to 0.21875
- latent_init: bfloat16 [256, 1280], replicated, may hold values from -6 to 6
- gain_latent: bfloat16 [1280], replicated, may hold values from 0.5 to 1.5
- query_enc: bfloat16 [1280, 256], replicated, may hold values from -0.15625 to 0.15625
- out_enc: bfloat16 [1280, 1280], replicated, may hold values from -0.625 to 0.625
- gain_enc_mlp: bfloat16 [1280], replicated, may hold values from 0.5 to 1.5
- up_enc: bfloat16 [1280, 1280], replicated, may hold values from -0.15625 to 0.15625
- down_enc: bfloat16 [1280, 1280], replicated, may hold values from -0.25 to 0.25
- gain_self: bfloat16 [1280], replicated, may hold values from 0.5 to 1.5
- query_self: bfloat16 [1280, 256], replicated, may hold values from -0.15625 to 0.15625
- key_self: bfloat16 [1280, 256], replicated, may hold values from -0.15625 to 0.15625
- value_self: bfloat16 [1280, 1280], replicated, may hold values from -0.15625 to 0.15625
- out_self: bfloat16 [1280, 1280], replicated, may hold values from -0.5 to 0.5
- gain_self_mlp: bfloat16 [1280], replicated, may hold values from 0.5 to 1.5
- up_self: bfloat16 [1280, 1280], replicated, may hold values from -0.15625 to 0.15625
- down_self: bfloat16 [1280, 1280], replicated, may hold values from -0.25 to 0.25
- gain_dec_kv: bfloat16 [1280], replicated, may hold values from 0.5 to 1.5
- key_dec: bfloat16 [1280, 256], replicated, may hold values from -0.15625 to 0.15625
- value_dec: bfloat16 [1280, 768], replicated, may hold values from -0.15625 to 0.15625
- dec_query: bfloat16 [2048, 768], replicated, may hold values from -6 to 6
- gain_dec_q: bfloat16 [768], replicated, may hold values from 0.5 to 1.5
- query_dec: bfloat16 [768, 256], replicated, may hold values from -0.21875 to 0.21875
- out_dec: bfloat16 [768, 768], replicated, may hold values from -0.625 to 0.625
- gain_final: bfloat16 [768], replicated, may hold values from 0.5 to 1.5
- logit_cot: bfloat16 [32, 2048, 262], P('items', 'blk'), may hold values from -6 to 6
Outputs:
- logits: bfloat16 [32, 2048, 262], P('items', 'blk')
- grad_embedding: float32 [262, 768], P(None, ('items', 'blk'))
- grad_position: float32 [2048, 768], P(('items', 'blk'))
- grad_mask_vector: float32 [768], P(('items', 'blk'))
- grad_gain_bytes: float32 [768], P(('items', 'blk'))
- grad_key_enc: float32 [768, 256], P(('items', 'blk'))
- grad_value_enc: float32 [768, 1280], P(('items', 'blk'))
- grad_latent_init: float32 [256, 1280], P(('items', 'blk'))
- grad_gain_latent: float32 [1280], P(('items', 'blk'))
- grad_query_enc: float32 [1280, 256], P(('items', 'blk'))
- grad_out_enc: float32 [1280, 1280], P(('items', 'blk'))
- grad_gain_enc_mlp: float32 [1280], P(('items', 'blk'))
- grad_up_enc: float32 [1280, 1280], P(('items', 'blk'))
- grad_down_enc: float32 [1280, 1280], P(('items', 'blk'))
- grad_gain_self: float32 [1280], P(('items', 'blk'))
- grad_query_self: float32 [1280, 256], P(('items', 'blk'))
- grad_key_self: float32 [1280, 256], P(('items', 'blk'))
- grad_value_self: float32 [1280, 1280], P(('items', 'blk'))
- grad_out_self: float32 [1280, 1280], P(('items', 'blk'))
- grad_gain_self_mlp: float32 [1280], P(('items', 'blk'))
- grad_up_self: float32 [1280, 1280], P(('items', 'blk'))
- grad_down_self: float32 [1280, 1280], P(('items', 'blk'))
- grad_gain_dec_kv: float32 [1280], P(('items', 'blk'))
- grad_key_dec: float32 [1280, 256], P(('items', 'blk'))
- grad_value_dec: float32 [1280, 768], P(('items', 'blk'))
- grad_dec_query: float32 [2048, 768], P(('items', 'blk'))
- grad_gain_dec_q: float32 [768], P(('items', 'blk'))
- grad_query_dec: float32 [768, 256], P(('items', 'blk'))
- grad_out_dec: float32 [768, 768], P(('items', 'blk'))
- grad_gain_final: float32 [768], P(('items', 'blk'))
Inputs may be any that keep to these rules, and one draw needn't show every extreme that they name: `span_start`: span s of an item lies inside bytes s * 256 to (s + 1) * 256 - 1; all spans of one item have the same length. `span_len`: between 5 and 50 percent of each item's bytes are masked.
All inputs are finite; a program needn't handle non-finite values.
Results may differ from a plain program's by a relative error of at most 0.02.
Values may be sent and summed in bfloat16 or wider, within the bound.
A program may use at most 384 MiB of HBM per device.

v0:
```python
import jax
import jax.numpy as jnp
from jax import lax
from jax.experimental import pallas as pl
from jax.experimental.pallas import tpu as pltpu
from jax.sharding import PartitionSpec as P

HEADS = 8
EPS = 1e-05
F32 = jnp.float32
BF16 = jnp.bfloat16
GELU_C = 0.7978845608028654
GELU_A = 0.044715


def nn(a, b):
    return lax.dot_general(a, b, (((1,), (0,)), ((), ())), preferred_element_type=F32)


def nt(a, b):
    return lax.dot_general(a, b, (((1,), (1,)), ((), ())), preferred_element_type=F32)


def tn(a, b):
    return lax.dot_general(a, b, (((0,), (0,)), ((), ())), preferred_element_type=F32)


def norm_forward(x, gain):
    centered = x - jnp.mean(x, axis=-1, keepdims=True)
    variance = jnp.mean(centered * centered, axis=-1, keepdims=True)
    rstd = lax.rsqrt(variance + EPS)
    hat = centered * rstd
    return (hat * gain.astype(F32)).astype(BF16), hat, rstd


def norm_backward(dy, hat, rstd, gain):
    dgain = jnp.sum(dy * hat, axis=0, keepdims=True)
    dhat = dy * gain.astype(F32)
    first = jnp.mean(dhat, axis=-1, keepdims=True)
    second = jnp.mean(dhat * hat, axis=-1, keepdims=True)
    return rstd * (dhat - first - hat * second), dgain


def gelu_forward(u):
    t = jnp.tanh(GELU_C * (u + GELU_A * u * u * u))
    return (0.5 * u * (1.0 + t)).astype(BF16)


def gelu_backward(dh, u):
    t = jnp.tanh(GELU_C * (u + GELU_A * u * u * u))
    slope = 0.5 * (1.0 + t) + 0.5 * u * (1.0 - t * t) * GELU_C * (1.0 + 3.0 * GELU_A * u * u)
    return dh * slope


def softmax(s):
    e = jnp.exp(s - jnp.max(s, axis=-1, keepdims=True))
    return e / jnp.sum(e, axis=-1, keepdims=True)


def softmax_backward(dp, soft, scale):
    inner = jnp.sum(dp * soft, axis=-1, keepdims=True)
    return (soft * (dp - inner) * scale).astype(BF16)


class Reducer:
    def __init__(self):
        n_items = lax.axis_size("items")
        self.count = n_items * lax.axis_size("blk")
        self.k = n_items.bit_length() - 1
        self.n_items = n_items

    def bit(self, name):
        if name == "y":
            return lax.axis_index("blk")
        return (lax.axis_index("items") >> name) & 1

    def exchange(self, x, name):
        if name == "y":
            return lax.ppermute(x, "blk", [(0, 1), (1, 0)])
        return lax.ppermute(x, "items", [(i, i ^ (1 << name)) for i in range(self.n_items)])

    def split(self, g):
        rows, width = g.shape
        return g.astype(BF16).reshape((2,) * (self.k + 1) + (rows // self.count, width))

    def reduce(self, grads, order):
        dims = list(range(self.k - 1, -1, -1)) + ["y"]
        parts = [self.split(g) for g in grads]
        heights = [p.shape[-2] for p in parts]
        for number, name in enumerate(order):
            axis = dims.index(name)
            mine = self.bit(name)
            send = [lax.dynamic_index_in_dim(p, 1 - mine, axis, keepdims=False) for p in parts]
            keep = [lax.dynamic_index_in_dim(p, mine, axis, keepdims=False) for p in parts]
            if number == 0:
                send = [jnp.concatenate(send, axis=-2)] if len(send) > 1 else send
                keep = [jnp.concatenate(keep, axis=-2)] if len(keep) > 1 else keep
            got = self.exchange(send[0], name)
            total = keep[0].astype(F32) + got.astype(F32)
            last = number == len(order) - 1
            parts = [total if last else total.astype(BF16)]
            dims.pop(axis)
        out, at = [], 0
        for height in heights:
            out.append(parts[0][at : at + height])
            at += height
        return out


CHUNK = 256
LAG = 2
MESH = pl.DeviceIdType.MESH
STAGES = {
    "xy": ("c", "x", "y", "z0", "z1"),
    "yx": ("c", "y", "x", "z0", "z1"),
}
ITEM_BIT = {"c": 0, "x": 1, "z0": 2, "z1": 3}


def padded_rows(r):
    return -(-r // 16) * 16


def my_bit(name):
    if name == "y":
        return lax.axis_index("blk")
    return (lax.axis_index("items") // 2 ** ITEM_BIT[name]) % 2


def partner(name):
    if name == "y":
        return {"blk": 1 - lax.axis_index("blk")}
    return {"items": lax.axis_index("items") + (1 - 2 * my_bit(name)) * 2 ** ITEM_BIT[name]}


def divide(first, second, mine, r, by_rows):
    if by_rows:
        first, second = (
            jnp.concatenate([first[:r], second[:r]], axis=0),
            jnp.concatenate([first[r:], second[r:]], axis=0),
        )
    return jnp.where(mine == 0, first, second), jnp.where(mine == 0, second, first)


def tie(values, after):
    count = len(values)
    anywhere = pl.BlockSpec(memory_space=pl.ANY)
    return pl.pallas_call(
        lambda *refs: None,
        out_shape=[jax.ShapeDtypeStruct(v.shape, v.dtype) for v in values],
        in_specs=[anywhere] * (count + len(after)),
        out_specs=[anywhere] * count,
        input_output_aliases={i: i for i in range(count)},
    )(*values, *after)


class Chunk:
    def __init__(self, bufs, at, sems, r, width, order):
        self.rc, self.r1, self.r2, self.r3, self.s4, self.r4, self.out = [b.at[at] for b in bufs]
        self.send, self.recv, self.at = sems[0], sems[1], at
        self.r, self.width, self.order = r, width, order
        self.step = 256 if r <= 40 and width % 256 == 0 else 128

    def copy(self, stage, source=None):
        src, dst = (
            (source, self.rc),
            (self.rc.at[:, :, 1], self.r1),
            (self.rc.at[:, 1, 0], self.r2),
            (self.rc.at[1, 0, 0], self.r3),
            (self.s4, self.r4),
        )[stage]
        return pltpu.make_async_remote_copy(
            src_ref=dst if src is None else src,
            dst_ref=dst,
            send_sem=self.send.at[self.at, stage],
            recv_sem=self.recv.at[self.at, stage],
            device_id=partner(STAGES[self.order][stage]),
            device_id_type=MESH,
        )

    def loop(self, pairs, body):
        columns = self.width // self.step

        def run(i, carry):
            body(i // columns, pl.ds(pl.multiple_of((i % columns) * self.step, self.step), self.step))
            return carry

        lax.fori_loop(0, pairs * columns, run, 0)

    def advance(self, stage, loaded=None):
        self.copy(stage).wait_recv()
        names = STAGES[self.order]
        r, kind, rc = self.r, self.rc.dtype, self.rc
        mine = my_bit(names[stage + 1]) if stage < 4 else None

        def total(a, b):
            return a.astype(F32) + b.astype(F32)

        def stage0(p, cols):
            q, z = p // 2, p % 2
            first = total(rc[q, z, 0, :, cols], loaded[q, z, 0, :, cols])
            second = total(rc[q, z, 1, :, cols], loaded[q, z, 1, :, cols])
            keep, send = divide(first, second, mine, r, names[1] == "y")
            rc[q, z, 0, :, cols] = keep.astype(kind)
            rc[q, z, 1, :, cols] = send.astype(kind)

        def stage1(q, cols):
            first = total(rc[q, 0, 0, :, cols], self.r1[q, 0, :, cols])
            second = total(rc[q, 1, 0, :, cols], self.r1[q, 1, :, cols])
            keep, send = divide(first, second, mine, r, True)
            rc[q, 0, 0, :, cols] = keep.astype(kind)
            rc[q, 1, 0, :, cols] = send.astype(kind)

        def stage2(q, cols):
            first = total(rc[0, 0, 0, :, cols], self.r2[0, :, cols])
            second = total(rc[1, 0, 0, :, cols], self.r2[1, :, cols])
            keep, send = divide(first, second, mine, r, True)
            rc[0, 0, 0, :, cols] = keep.astype(kind)
            rc[1, 0, 0, :, cols] = send.astype(kind)

        def stage3(q, cols):
            both = total(rc[0, 0, 0, :, cols], self.r3[:, cols])
            keep = jnp.where(mine == 0, both[:r], both[r:])
            send = jnp.where(mine == 0, both[r:], both[:r])
            extra = padded_rows(r) - r
            if extra:
                send = jnp.concatenate([send, jnp.zeros((extra, send.shape[1]), F32)], axis=0)
            self.s4[:, cols] = send.astype(kind)
            self.out[:, cols] = keep

        def stage4(q, cols):
            self.out[:, cols] = self.out[:, cols] + self.r4[:, cols].astype(F32)[:r]

        self.loop((4, 2, 1, 1, 1)[stage], (stage0, stage1, stage2, stage3, stage4)[stage])
        if stage < 4:
            self.copy(stage + 1).start()


def when(condition, action):
    if isinstance(condition, bool):
        if condition:
            action()
    else:
        pl.when(condition)(action)


SLOTS = 4
AHEAD = 3
B_SLOTS = 3


def reduce_kernel(plan, *refs):
    sides, steps, n_act, n_cot, widths, others = plan
    n_a, n_o = len(widths), len(others)
    acts, refs = refs[:n_act], refs[n_act:]
    cots, refs = refs[:n_cot], refs[n_cot:]
    o_src, refs = refs[:n_o], refs[n_o:]
    a_out, o_out = refs[:n_a], refs[n_a : n_a + n_o]
    refs = refs[n_a + n_o :]
    a_bufs, refs = refs[:7], refs[7:]
    act_in, act_t, cot_in, made = refs[:4]
    refs = refs[4:]
    o_bufs, refs = [refs[8 * i : 8 * i + 8] for i in range(n_o)], refs[8 * n_o :]
    a_sems, o_sems = refs[0:2], refs[2:4]
    act_sem, cot_sem, o_load_sem, a_out_sem, o_out_sem = refs[4:]
    core = my_bit("c")
    rows = act_t.shape[1] // 4

    barrier = pltpu.get_barrier_semaphore()
    for name in ("c", "x", "y", "z0", "z1"):
        pl.semaphore_signal(barrier, inc=1, device_id=partner(name), device_id_type=MESH)
    pl.semaphore_wait(barrier, 5)

    def chunk(step, side):
        return Chunk(a_bufs, 2 * step + side, a_sems, 40, CHUNK, ("xy", "yx")[side])

    def act_copy(side, group):
        return pltpu.make_async_copy(acts[sides[side][0][group][1]], act_in.at[side], act_sem.at[side])

    def cot_copy(side, step):
        source, number, _ = sides[side][1][step]
        slot = step % B_SLOTS
        return pltpu.make_async_copy(
            cots[source].at[:, pl.ds(number * CHUNK, CHUNK)], cot_in.at[side, slot], cot_sem.at[side, slot]
        )

    def first_copy(step, side):
        return chunk(step, side).copy(0, made.at[side, step % SLOTS, 1 - core])

    def produce(step):
        for side in range(2):
            groups = sides[side][0]
            for g, (start, _) in enumerate(groups):

                def fresh(g=g, side=side, groups=groups):
                    act_copy(side, g).wait()

                    def turn(i, carry):
                        at = pl.ds(pl.multiple_of(i * 256, 256), 256)
                        act_t[side, at, :] = act_in[side, :, at].T
                        return carry

                    lax.fori_loop(0, act_in.shape[2] // 256, turn, 0)
                    if g + 1 < len(groups):
                        act_copy(side, g + 1).start()

                when(step == start, fresh)
            for later in range(B_SLOTS - 1, steps):
                when(step == later - (B_SLOTS - 1), lambda later=later, side=side: cot_copy(side, later).start())
            slot = step % B_SLOTS
            pltpu.make_async_copy(
                cots[0].at[:, pl.ds(0, CHUNK)], cot_in.at[side, slot], cot_sem.at[side, slot]
            ).wait()
            when(step >= SLOTS, lambda side=side: first_copy(step - SLOTS, side).wait_send())

            def product(i, carry, side=side, slot=slot):
                part = act_t[side, pl.ds(pl.multiple_of(i * rows, rows), rows), :]
                result = jnp.dot(part, cot_in[side, slot], preferred_element_type=F32)
                height = rows // 4
                for x in range(2):
                    for c in range(2):
                        at = (2 * x + c) * height
                        made[side, step % SLOTS, c, i // 2, i % 2, x] = result[at : at + height].astype(BF16)
                return carry

            lax.fori_loop(0, 4, product, 0)
            first_copy(step, side).start()

    small = []
    for i, (r, width, order) in enumerate(others):
        item = Chunk([b.at[0:1] for b in o_bufs[i][:7]], 0, o_sems, r, width, order)
        item.at = i
        small.append(item)
        item.copy(0, o_src[i].at[:, :, :, 1 - core]).start()
        pltpu.make_async_copy(o_src[i].at[:, :, :, core], o_bufs[i][7], o_load_sem.at[i]).start()
    for side in range(2):
        act_copy(side, 0).start()
        for step in range(B_SLOTS - 1):
            cot_copy(side, step).start()

    def begin(step, carry):
        produce(step)
        return carry

    lax.fori_loop(0, AHEAD, begin, 0)
    for i, item in enumerate(small):
        pltpu.make_async_copy(o_src[i].at[:, :, :, core], o_bufs[i][7], o_load_sem.at[i]).wait()
        item.advance(0, o_bufs[i][7])

    def run(step, carry):
        pl.when(step + AHEAD < steps)(lambda: produce(step + AHEAD))

        def enter():
            for side in range(2):
                chunk(step, side).advance(0, made.at[side, step % SLOTS, core])

        pl.when(step < steps)(enter)
        for stage in range(4, 0, -1):
            old = step - stage * LAG

            def act(old=old, stage=stage):
                for side in range(2):
                    chunk(old, side).advance(stage)

            pl.when(jnp.logical_and(old >= 0, old < steps))(act)
        for number in range(4):

            def others_on(number=number):
                for item in small:
                    item.advance(number + 1)

            pl.when(step == 4 + 5 * number)(others_on)
        return carry

    lax.fori_loop(0, steps + 4 * LAG, run, 0)

    outs = []
    for side in range(2):
        for step in range(steps):
            _, number, target = sides[side][1][step]
            at = 2 * step + side
            outs.append(
                pltpu.make_async_copy(
                    a_bufs[6].at[at], a_out[target].at[:, pl.ds(number * CHUNK, CHUNK)], a_out_sem.at[at]
                )
            )
    for i in range(n_o):
        outs.append(pltpu.make_async_copy(o_bufs[i][6].at[0], o_out[i], o_out_sem.at[i]))
    for copy in outs:
        copy.start()
    for step in range(steps - SLOTS, steps):
        for side in range(2):
            first_copy(step, side).wait_send()
    for i, item in enumerate(small):
        item.copy(0, o_src[i].at[:, :, :, 1 - core]).wait_send()
        for stage in range(1, 5):
            item.copy(stage).wait_send()

    def wait_sent(step, carry):
        for side in range(2):
            for stage in range(1, 5):
                chunk(step, side).copy(stage).wait_send()
        return carry

    lax.fori_loop(0, steps, wait_sent, 0)
    for copy in outs:
        copy.wait()


def buffers(count, r, width, kind):
    rp = padded_rows(r)
    return [
        pltpu.VMEM((count, 2, 2, 2, 2 * r, width), kind),
        pltpu.VMEM((count, 2, 2, 2 * r, width), kind),
        pltpu.VMEM((count, 2, 2 * r, width), kind),
        pltpu.VMEM((count, 2 * r, width), kind),
        pltpu.VMEM((count, rp, width), kind),
        pltpu.VMEM((count, rp, width), kind),
        pltpu.VMEM((count, r, width), F32),
    ]


def reduce_all(products, others):
    acts, cots, sides, widths = [], [], [], []
    for side in products:
        groups, sequence = [], []
        for act, own in side:
            groups.append((len(sequence), len(acts)))
            acts.append(act)
            for cot in own:
                for number in range(cot.shape[1] // CHUNK):
                    sequence.append((len(cots), number, len(widths)))
                cots.append(cot)
                widths.append(cot.shape[1])
        sides.append((tuple(groups), tuple(sequence)))
    steps = len(sides[0][1])
    assert steps == len(sides[1][1])

    def view(g):
        return g.reshape(2, 2, 2, 2, g.shape[0] // 16, g.shape[1])

    plan = (
        tuple(sides), steps, len(acts), len(cots), tuple(widths),
        tuple((g.shape[0] // 32, g.shape[1], order) for g, order in others),
    )
    depth, features = acts[0].shape
    scratch = buffers(2 * steps, 40, CHUNK, BF16)
    scratch += [
        pltpu.VMEM((2, depth, features), BF16),
        pltpu.VMEM((2, features, depth), BF16),
        pltpu.VMEM((2, B_SLOTS, depth, CHUNK), BF16),
        pltpu.VMEM((2, SLOTS, 2, 2, 2, 2, 80, CHUNK), BF16),
    ]
    for g, order in others:
        r = g.shape[0] // 32
        scratch += buffers(1, r, g.shape[1], g.dtype)
        scratch.append(pltpu.VMEM((2, 2, 2, 2 * r, g.shape[1]), g.dtype))
    dma = pltpu.SemaphoreType.DMA
    scratch += [dma((2 * steps, 5)), dma((2 * steps, 5)), dma((len(others), 5)), dma((len(others), 5))]
    scratch += [dma((2,)), dma((2, B_SLOTS)), dma((len(others),)), dma((2 * steps,)), dma((len(others),))]
    anywhere = pl.BlockSpec(memory_space=pl.ANY)
    arrays = acts + cots + [view(g) for g, order in others]
    results = pl.pallas_call(
        lambda *refs: reduce_kernel(plan, *refs),
        out_shape=[jax.ShapeDtypeStruct((features // 32, w), F32) for w in widths]
        + [jax.ShapeDtypeStruct((g.shape[0] // 32, g.shape[1]), F32) for g, order in others],
        in_specs=[anywhere] * len(arrays),
        out_specs=[anywhere] * (len(widths) + len(others)),
        scratch_shapes=scratch,
        compiler_params=pltpu.CompilerParams(
            collective_id=0, has_side_effects=True, vmem_limit_bytes=62 * 1024 * 1024
        ),
    )(*arrays)
    return results[: len(widths)], results[len(widths) :]


def finish(plain, table, vectors, vocab, vector_count):
    count = len(plain)
    width = table.shape[0]

    def kernel(*refs):
        sources, refs = refs[:count], refs[count:]
        table_ref, vectors_ref = refs[:2]
        refs = refs[2:]
        targets, refs = refs[:count], refs[count:]
        emb_ref, row_refs, refs = refs[0], refs[1:5], refs[5:]
        gain_refs, refs = refs[:vector_count], refs[vector_count:]
        staged, (in_sem, out_sem) = refs[:count], refs[count:]
        inward = [pltpu.make_async_copy(sources[i], staged[i], in_sem.at[i]) for i in range(count)]
        outward = [pltpu.make_async_copy(staged[i], targets[i], out_sem.at[i]) for i in range(count)]
        for copy in inward:
            copy.start()
        turned = table_ref[...].T
        emb_ref[...] = table_ref[:, :vocab]
        vector_rows = vectors_ref[...].T
        for i, row_ref in enumerate(row_refs):
            row_ref[...] = turned[vocab + i]
        for i, gain_ref in enumerate(gain_refs):
            gain_ref[...] = vector_rows[i]
        for i in range(count):
            inward[i].wait()
            outward[i].start()
        for copy in outward:
            copy.wait()

    anywhere = pl.BlockSpec(memory_space=pl.ANY)
    local_memory = pl.BlockSpec(memory_space=pltpu.VMEM)
    shapes = [jax.ShapeDtypeStruct(p.shape, F32) for p in plain]
    shapes += [jax.ShapeDtypeStruct((width, vocab), F32)] + [jax.ShapeDtypeStruct((width,), F32)] * 4
    shapes += [jax.ShapeDtypeStruct(vectors.shape[:1], F32)] * vector_count
    results = pl.pallas_call(
        kernel,
        out_shape=shapes,
        in_specs=[anywhere] * count + [local_memory] * 2,
        out_specs=[anywhere] * count + [local_memory] * (5 + vector_count),
        scratch_shapes=[pltpu.VMEM(p.shape, F32) for p in plain] + [pltpu.SemaphoreType.DMA((count,))] * 2,
    )(*plain, table, vectors)
    return results[:count], results[count], results[count + 1 : count + 5], results[count + 5 :]


def center(x):
    hat = x - jnp.mean(x, axis=-1, keepdims=True)
    rstd = lax.rsqrt(jnp.mean(hat * hat, axis=-1, keepdims=True) + EPS)
    return hat * rstd, rstd


def center_backward(dhat, hat, rstd):
    first = jnp.mean(dhat, axis=-1, keepdims=True)
    second = jnp.mean(dhat * hat, axis=-1, keepdims=True)
    return rstd * (dhat - first - hat * second)


def decoder_kernel(
    scale, query, cot, emb, key, value, w_query, w_out, gain_q, gain_f,
    logits, dquery, g_emb, g_gains, dkey, dvalue, g_query, g_out,
    g_pd, g_dn, kq, vo, vo_mid,
):
    @pl.when(pl.program_id(0) == 0)
    def _():
        for ref in (g_emb, g_pd, g_dn, g_gains):
            ref[...] = jnp.zeros_like(ref)
        kq[...] = nt(key[...], w_query[...]).astype(BF16)
        out = nn(value[...], w_out[...])
        vo[...] = out.astype(BF16)
        vo_mid[...] = (out - jnp.mean(out, axis=0, keepdims=True)).astype(BF16)

    x = query[...].astype(F32)
    hat_q, rstd_q = center(x)
    gq, gf = gain_q[...].astype(F32), gain_f[...].astype(F32)
    nq = (hat_q * gq).astype(BF16)
    soft = softmax(nt(nq, kq[...]) * scale)
    p = soft.astype(BF16)
    hat_f, rstd_f = center(x + nn(p, vo[...]))
    nf = (hat_f * gf).astype(BF16)
    logits[...] = nt(emb[...], nf).astype(BF16)
    dnf = nn(cot[...].T, emb[...])
    g_emb[...] += nn(cot[...], nf)
    g_gains[0:1] += jnp.sum(dnf * hat_f, axis=0, keepdims=True)
    ddec = center_backward(dnf * gf, hat_f, rstd_f)
    ddec16 = ddec.astype(BF16)
    g_pd[...] += nn(p.T, ddec16)
    ds = softmax_backward(nt(ddec16, vo_mid[...]), soft, scale)
    g_dn[...] += nn(ds.T, nq)
    dnq = nn(ds, kq[...])
    g_gains[1:2] += jnp.sum(dnq * hat_q, axis=0, keepdims=True)
    dquery[...] = (ddec + center_backward(dnq * gq, hat_q, rstd_q)).astype(BF16)

    @pl.when(pl.program_id(0) == pl.num_programs(0) - 1)
    def _():
        pd, dn = g_pd[...].astype(BF16), g_dn[...].astype(BF16)
        dvalue[...] = nt(pd, w_out[...]).astype(BF16)
        dkey[...] = nn(dn, w_query[...]).astype(BF16)
        g_out[...] = nn(value[...].T, pd).astype(BF16)
        g_query[...] = nn(dn.T, key[...]).astype(BF16)


def decoder_pass(query, cot, emb, key, value, w_query, w_out, gain_q, gain_f, scale):
    rows, width = query.shape
    vocab, latents, block = emb.shape[0], key.shape[0], 512

    def whole(x):
        return pl.BlockSpec(x.shape, lambda i: (0, 0))

    sums = jax.ShapeDtypeStruct((latents, width), F32)
    shapes = [
        jax.ShapeDtypeStruct((vocab, rows), BF16),
        jax.ShapeDtypeStruct((rows, width), BF16),
        jax.ShapeDtypeStruct((vocab, width), F32),
        jax.ShapeDtypeStruct((8, width), F32),
    ] + [jax.ShapeDtypeStruct(x.shape, BF16) for x in (key, value, w_query, w_out)]
    small = (gain_q[None, :], gain_f[None, :])
    return pl.pallas_call(
        lambda *refs: decoder_kernel(scale, *refs),
        grid=(rows // block,),
        out_shape=shapes,
        in_specs=[
            pl.BlockSpec((block, width), lambda i: (i, 0)),
            pl.BlockSpec((vocab, block), lambda i: (0, i)),
        ]
        + [whole(x) for x in (emb, key, value, w_query, w_out) + small],
        out_specs=[
            pl.BlockSpec((vocab, block), lambda i: (0, i)),
            pl.BlockSpec((block, width), lambda i: (i, 0)),
        ]
        + [whole(x) for x in shapes[2:]],
        scratch_shapes=[pltpu.VMEM(sums.shape, F32)] * 2 + [pltpu.VMEM(sums.shape, BF16)] * 3,
        compiler_params=pltpu.CompilerParams(vmem_limit_bytes=56 * 1024 * 1024),
    )(query, cot, emb, key, value, w_query, w_out, *small)


def bytes_kernel(
    at, scale, p, soft, vd, qk, nb, rstd, gain, codes, emb, sums, wide,
    pn, q, dae, daft, nl, rstd_l, gain_l, w_key, w_query,
    dbytes, table, turned, dq, g_key, g_value, g_latent,
    total, ds,
):
    i = pl.program_id(0)
    block = codes.shape[1]

    @pl.when(i == 0)
    def _():
        total[...] = jnp.zeros_like(total)
        total[: emb.shape[0]] = emb[...]
        total[at + 1 : at + 2] = sums[1:2]
        total[at + 2 : at + 3] = sums[0:1]
        ds[...] = softmax_backward(nt(vd[...], nb[...]), soft[...], scale)
        dn = nn(ds[...], nb[...]).astype(BF16)
        g_key[...] = nn(dn.T, q[...]).astype(BF16)
        g_value[...] = nn(pn[...].T, dae[...]).astype(BF16)
        dq[...] = nn(dn, w_key[...]).astype(BF16)
        dnl = nt(dq[...], w_query[...])
        g = gain_l[...].astype(F32)
        hat = nl[...].astype(F32) / g
        g_latent[...] = (daft[...] + center_backward(dnl * g, hat, rstd_l[...])).astype(BF16)
        first = jnp.sum(dnl * hat, axis=0, keepdims=True)
        own = lax.broadcasted_iota(jnp.int32, wide.shape, 0) == 0
        turned[...] = jnp.zeros_like(turned)
        turned[:, : wide.shape[0]] = jnp.where(own, first, wide[...]).T.astype(BF16)

    rows = pl.ds(pl.multiple_of(i * block, block), block)
    g = gain[...].astype(F32)
    normed = nb[rows, :]
    dnb = nn(p[...].T, vd[...]) + nn(ds[:, rows].T, qk[...])
    hat = normed.astype(F32) / g
    dx = center_backward(dnb * g, hat, rstd[...]).astype(BF16)
    dbytes[...] = dx
    entry = lax.broadcasted_iota(jnp.int32, (total.shape[0], block), 0)
    onehot = (entry == codes[...]).astype(BF16)
    total[...] += nn(onehot, dx)
    total[at : at + 1] += jnp.sum(dnb * hat, axis=0, keepdims=True)

    @pl.when(i == pl.num_programs(0) - 1)
    def _():
        table[...] = total[...].T.astype(BF16)


def bytes_backward(at, scale, p, soft, vd, qk, nb, rstd, gain, codes, emb, sums, wide, rest):
    rows, width = nb.shape
    latents, block, entries = p.shape[0], 256, -(-emb.shape[0] // 128) * 128
    features = wide.shape[1]
    qk_width = rest[1].shape[1]

    def whole(x):
        return pl.BlockSpec(x.shape, lambda i: (0, 0))

    shapes = [
        jax.ShapeDtypeStruct((rows, width), BF16),
        jax.ShapeDtypeStruct((width, entries), BF16),
        jax.ShapeDtypeStruct((features, 128), BF16),
        jax.ShapeDtypeStruct((latents, qk_width), BF16),
        jax.ShapeDtypeStruct((width, qk_width), BF16),
        jax.ShapeDtypeStruct((width, features), BF16),
        jax.ShapeDtypeStruct((latents, features), BF16),
    ]
    arrays = (p, soft, vd, qk, nb, rstd, gain[None, :], codes[None, :], emb, sums, wide) + rest
    specs = [whole(x) for x in arrays]
    specs[0] = pl.BlockSpec((latents, block), lambda i: (0, i))
    specs[5] = pl.BlockSpec((block, 1), lambda i: (i, 0))
    specs[7] = pl.BlockSpec((1, block), lambda i: (0, i))
    return pl.pallas_call(
        lambda *refs: bytes_kernel(at, scale, *refs),
        grid=(rows // block,),
        out_shape=shapes,
        in_specs=specs,
        out_specs=[pl.BlockSpec((block, width), lambda i: (i, 0))] + [whole(x) for x in shapes[1:]],
        scratch_shapes=[pltpu.VMEM((entries, width), F32), pltpu.VMEM((latents, rows), BF16)],
        compiler_params=pltpu.CompilerParams(vmem_limit_bytes=60 * 1024 * 1024),
    )(*arrays)


def head_columns(head, width):
    each = width // HEADS
    low, high = head * each // 128 * 128, -(-(head + 1) * each // 128) * 128
    place = low + lax.broadcasted_iota(jnp.int32, (1, high - low), 1)
    return slice(low, high), jnp.logical_and(place >= head * each, place < (head + 1) * each)


def pick(mask, x):
    return jnp.where(mask, x, jnp.zeros_like(x))


def head_softmax(head, q, k):
    columns, mask = head_columns(head, q.shape[1])
    scale = (q.shape[1] // HEADS) ** (-0.5)
    return softmax(nt(pick(mask, q[:, columns]), k[:, columns]) * scale), scale


def self_forward_heads(q, k, v, total):
    total[...] = jnp.zeros_like(total)
    for head in range(HEADS):
        p = head_softmax(head, q, k)[0].astype(BF16)
        columns, mask = head_columns(head, v.shape[1])
        total[:, columns] += nn(p, pick(mask, v[:, columns]))


def self_backward_heads(q, k, v, da, dq_sum, dk_sum, dv_sum):
    for ref in (dq_sum, dk_sum, dv_sum):
        ref[...] = jnp.zeros_like(ref)
    for head in range(HEADS):
        soft, scale = head_softmax(head, q, k)
        columns, mask = head_columns(head, v.shape[1])
        da_head = pick(mask, da[:, columns])
        ds = softmax_backward(nt(da_head, v[:, columns]), soft, scale)
        dv_sum[:, columns] += nn(soft.astype(BF16).T, da_head)
        columns, mask = head_columns(head, q.shape[1])
        dq_sum[:, columns] += nn(ds, pick(mask, k[:, columns]))
        dk_sum[:, columns] += nn(ds.T, pick(mask, q[:, columns]))


class Stream:
    def __init__(self, sources, targets, sem):
        self.copies = [pltpu.make_async_copy(a, b, sem.at[i]) for i, (a, b) in enumerate(zip(sources, targets))]
        self.targets, self.arrived = targets, set()
        for copy in self.copies:
            copy.start()

    def __getitem__(self, i):
        if i not in self.arrived:
            self.copies[i].wait()
            self.arrived.add(i)
        return self.targets[i][...]


class Results:
    def __init__(self, stage, targets, sem):
        self.stage, self.targets, self.sem, self.copies = stage, targets, sem, []

    def put(self, value):
        i = len(self.copies)
        self.stage[i][...] = value.astype(self.stage[i].dtype)
        copy = pltpu.make_async_copy(self.stage[i], self.targets[i], self.sem.at[i])
        copy.start()
        self.copies.append(copy)
        return self.stage[i]

    def finish(self):
        for copy in self.copies:
            copy.wait()


def streamed(body, small, large, shapes, extra):
    n_s, n_l, n_o = len(small), len(large), len(shapes)

    def kernel(*refs):
        ins, refs = refs[: n_s + n_l], refs[n_s + n_l :]
        outs, refs = refs[:n_o], refs[n_o:]
        held, refs = refs[:n_l], refs[n_l:]
        stage, refs = refs[:n_o], refs[n_o:]
        stream = Stream(ins[n_s:], held, refs[0])
        results = Results(stage, outs, refs[1])
        body(ins[:n_s], stream, results, refs[2:])
        results.finish()

    anywhere = pl.BlockSpec(memory_space=pl.ANY)
    return pl.pallas_call(
        kernel,
        out_shape=shapes,
        in_specs=[pl.BlockSpec(memory_space=pltpu.VMEM)] * n_s + [anywhere] * n_l,
        out_specs=[anywhere] * n_o,
        scratch_shapes=[pltpu.VMEM(x.shape, x.dtype) for x in large]
        + [pltpu.VMEM(x.shape, x.dtype) for x in shapes]
        + [pltpu.SemaphoreType.DMA((n_l,)), pltpu.SemaphoreType.DMA((n_o,))]
        + extra,
        compiler_params=pltpu.CompilerParams(vmem_limit_bytes=60 * 1024 * 1024),
    )(*small, *large)


def spread(column):
    return jnp.broadcast_to(column, (column.shape[0], 128))


def latent_forward(latent, pn, gains, weights):
    rows, width = latent.shape
    wide, narrow = (rows, width), (rows, weights[4].shape[1])

    def body(small, w, results, extra):
        latent_ref, pn_ref, g1, g2, g3, g4 = small
        (total,) = extra
        put = results.put

        def norm(x, gain):
            hat, rstd = center(x)
            return put(hat * gain[...].astype(F32)), rstd

        a_e = put(nn(pn_ref[...], w[0]))
        x = latent_ref[...].astype(F32) + nn(a_e[...], w[1])
        n1, r1 = norm(x, g1)
        u1 = put(nn(n1[...], w[2]))
        h1 = put(gelu_forward(u1[...]))
        x = x + nn(h1[...], w[3])
        n2, r2 = norm(x, g2)
        q, k, v = put(nn(n2[...], w[4])), put(nn(n2[...], w[5])), put(nn(n2[...], w[6]))
        self_forward_heads(q, k, v, total)
        a_s = put(total[...])
        x = x + nn(a_s[...], w[7])
        n3, r3 = norm(x, g3)
        u2 = put(nn(n3[...], w[8]))
        h2 = put(gelu_forward(u2[...]))
        x = x + nn(h2[...], w[9])
        n4, r4 = norm(x, g4)
        put(nn(n4[...], w[10]))
        put(nn(n4[...], w[11]))
        for r in (r1, r2, r3, r4):
            put(spread(r))

    def low(shape):
        return jax.ShapeDtypeStruct(shape, BF16)

    full = jax.ShapeDtypeStruct(wide, F32)
    shapes = [low(wide), low(wide), full, low(wide), low(wide), low(narrow), low(narrow), low(wide)]
    shapes += [low(wide), low(wide), full, low(wide), low(wide)]
    shapes += [low((rows, weights[10].shape[1])), low((rows, weights[11].shape[1]))]
    shapes += [jax.ShapeDtypeStruct((rows, 128), F32)] * 4
    small = [latent, pn] + [g[None, :] for g in gains]
    return streamed(body, small, weights, shapes, [pltpu.VMEM(wide, F32)])


def latent_backward(dk_d, dv_d, gains, kept, weights):
    rows, width = kept[0].shape
    count = len(weights)

    def body(small, stream, results, extra):
        dk_ref, dv_ref, g1, g2, g3, g4 = small
        dq_sum, dk_sum, dv_sum, sums = extra
        put = results.put
        w = stream
        sums[...] = jnp.zeros_like(sums)

        def norm(dy, normed, rstd, gain, row):
            g = gain[...].astype(F32)
            hat = normed.astype(F32) / g
            sums[row : row + 1] = jnp.sum(dy * hat, axis=0, keepdims=True)
            return center_backward(dy * g, hat, rstd[:, :1])

        n4, u2, n3, q, k, v, n2, u1, n1, r4, r3, r2, r1 = range(count, count + 13)
        dlat = norm(nt(dk_ref[...], w[0]) + nt(dv_ref[...], w[1]), w[n4], w[r4], g4, 4)
        dlat16 = put(dlat)
        du2 = put(gelu_backward(nt(dlat16[...], w[2]), w[u2]))
        das = dlat + norm(nt(du2[...], w[3]), w[n3], w[r3], g3, 3)
        das16 = put(das)
        da = nt(das16[...], w[4]).astype(BF16)
        w[q], w[k], w[v]
        self_backward_heads(w.targets[q], w.targets[k], w.targets[v], da, dq_sum, dk_sum, dv_sum)
        dq, dk, dv = put(dq_sum[...]), put(dk_sum[...]), put(dv_sum[...])
        dn2 = nt(dq[...], w[5]) + nt(dk[...], w[6]) + nt(dv[...], w[7])
        denc = das + norm(dn2, w[n2], w[r2], g2, 2)
        denc16 = put(denc)
        du1 = put(gelu_backward(nt(denc16[...], w[8]), w[u1]))
        daft = denc + norm(nt(du1[...], w[9]), w[n1], w[r1], g1, 1)
        daft16 = put(daft)
        put(daft)
        dae = put(nt(daft16[...], w[10]))
        put(nt(dae[...], w[11]))
        put(sums[...])

    wide = (rows, width)
    low, narrow = jax.ShapeDtypeStruct(wide, BF16), jax.ShapeDtypeStruct(kept[3].shape, BF16)
    shapes = [low, low, low, narrow, narrow, low, low, low, low, jax.ShapeDtypeStruct(wide, F32), low]
    shapes += [jax.ShapeDtypeStruct((rows, weights[11].shape[0]), BF16), jax.ShapeDtypeStruct((8, width), F32)]
    extra = [pltpu.VMEM(x.shape, F32) for x in kept[3:6]] + [pltpu.VMEM((8, width), F32)]
    large = list(weights) + list(kept)
    order = [0, 1, count, count + 9, 2, count + 1, 3, count + 2, count + 10, 4, count + 3, count + 4, count + 5]
    order += [5, 6, 7, count + 6, count + 11, 8, count + 7, 9, count + 8, count + 12, 10, 11]
    place = {old: new for new, old in enumerate(order)}

    class Ordered:
        def __init__(self, stream):
            self.stream, self.targets = stream, {old: stream.targets[new] for old, new in place.items()}

        def __getitem__(self, i):
            return self.stream[place[i]]

    small = [dk_d, dv_d] + [g[None, :] for g in gains]
    return streamed(
        lambda a, b, c, d: body(a, Ordered(b), c, d), small, [large[i] for i in order], shapes, extra
    )


def local(
    byte_ids, span_start, span_len, embedding, position, mask_vector, gain_bytes, key_enc,
    value_enc, latent_init, gain_latent, query_enc, out_enc, gain_enc_mlp, up_enc, down_enc,
    gain_self, query_self, key_self, value_self, out_self, gain_self_mlp, up_self, down_self,
    gain_dec_kv, key_dec, value_dec, dec_query, gain_dec_q, query_dec, out_dec, gain_final,
    logit_cot,
):
    me = lax.axis_index("blk")
    half = byte_ids.shape[1]
    total = position.shape[0]
    vocab = embedding.shape[0]
    reducer = Reducer()
    k = reducer.k
    order_yx = [0, "y", 1] + list(range(2, k))
    order_xy = [0, 1, "y"] + list(range(2, k))

    def swap(x):
        return lax.ppermute(x, "blk", [(0, 1), (1, 0)])

    def own_item(first, second, after=()):
        mine = jnp.where(me == 0, first, second)
        send = jnp.where(me == 0, second, first)
        if after:
            (send,) = tie([send], after)
        got = swap(send)
        low_half = jnp.where(me == 0, mine, got)
        high_half = jnp.where(me == 0, got, mine)
        return jnp.concatenate([low_half, high_half], axis=-1)

    ids = own_item(byte_ids[0], byte_ids[1])
    cot_rows = logit_cot.transpose(2, 0, 1)
    cot = own_item(cot_rows[:, 0], cot_rows[:, 1], [ids])
    entries = -(-(vocab + 4) // 16) * 16
    cot = jnp.pad(cot, ((0, entries - vocab), (0, 0)))
    emb_rows = jnp.pad(embedding, ((0, entries - vocab), (0, 0)))
    starts = lax.dynamic_index_in_dim(span_start, me, 0, keepdims=False)
    lengths = lax.dynamic_index_in_dim(span_len, me, 0, keepdims=False)

    places = lax.iota(jnp.int32, total)
    inside = (places[None, :] >= starts[:, None]) & (places[None, :] < (starts + lengths)[:, None])
    codes = jnp.where(jnp.any(inside, axis=0), vocab, ids)
    padded = -(-(vocab + 4) // 128) * 128
    table = jnp.concatenate(
        [embedding, mask_vector[None, :], jnp.zeros((padded - vocab - 1, embedding.shape[1]), BF16)], axis=0
    )
    onehot = (codes[:, None] == lax.iota(jnp.int32, padded)[None, :]).astype(BF16)
    bytes_in = nn(onehot, table) + position.astype(F32)
    nb, hat_b, rstd_b = norm_forward(bytes_in, gain_bytes)

    latent32 = latent_init.astype(F32)
    nl, hat_l, rstd_l = norm_forward(latent32, gain_latent)
    q_e = nn(nl, query_enc).astype(BF16)
    scale_e = q_e.shape[1] ** (-0.5)
    qk_e = nt(q_e, key_enc).astype(BF16)
    soft_e = softmax(nt(qk_e, nb) * scale_e)
    p_e = soft_e.astype(BF16)
    pn_e = nn(p_e, nb).astype(BF16)
    gains = (gain_enc_mlp, gain_self, gain_self_mlp, gain_dec_kv)
    (
        a_e, n1, u1, h1, n2, q_s, k_s, v_s, a_s, n3, u2, h2, n4, k_d, v_d, rstd1, rstd2, rstd3, rstd4,
    ) = latent_forward(
        latent_init, pn_e, gains,
        [
            value_enc, out_enc, up_enc, down_enc, query_self, key_self, value_self, out_self, up_self,
            down_self, key_dec, value_dec,
        ],
    )

    scale_d = k_d.shape[1] ** (-0.5)
    logits, g_dec_query, g_emb_out, gain_sums, dk_d, dv_d, g_query_dec, g_out_dec = decoder_pass(
        dec_query, cot, emb_rows, k_d, v_d, query_dec, out_dec, gain_dec_q, gain_final, scale_d
    )
    logits = logits[:vocab]
    logits_got = swap(jnp.where(me == 0, logits[:, half:], logits[:, :half]))
    logits_own = jnp.where(me == 0, logits[:, :half], logits[:, half:])
    side = lax.broadcasted_iota(jnp.int32, (1, 2, 1), 1)
    logits_out = jnp.where(side == me, logits_own[:, None, :], logits_got[:, None, :]).transpose(1, 2, 0)

    dlat16, du2, das16, dq_s, dk_s, dv_s, denc16, du1, daft16, dafter, dae16, vd_e, wide = latent_backward(
        dk_d, dv_d, gains, [n4, u2, n3, q_s, k_s, v_s, n2, u1, n1, rstd4, rstd3, rstd2, rstd1],
        [
            key_dec, value_dec, down_self, up_self, out_self, query_self, key_self, value_self, down_enc,
            up_enc, out_enc, value_enc,
        ],
    )

    dbytes, g_table, vectors, dq_e, g_key_enc, g_value_enc, g_latent = bytes_backward(
        vocab + 1, scale_e, p_e, soft_e, vd_e, qk_e, nb, rstd_b, gain_bytes, codes, g_emb_out, gain_sums, wide,
        (pn_e, q_e, dae16, dafter, nl, rstd_l, gain_latent[None, :], key_enc, query_enc),
    )

    def low(g):
        return g.astype(BF16)

    if reducer.n_items == 16:
        first_side = [(n1, [du1]), (a_e, [daft16]), (n3, [du2]), (n2, [dv_s, dk_s])]
        second_side = [
            (h1, [denc16]), (h2, [dlat16]), (a_s, [das16]), (n4, [dv_d, dk_d]), (n2, [dq_s]), (nl, [dq_e]),
        ]
        others = [
            (low(g_dec_query), "xy"), (low(dbytes), "yx"), (low(g_value_enc), "xy"), (low(g_out_dec), "yx"),
            (low(g_table), "yx"), (low(g_key_enc), "xy"), (low(g_query_dec), "yx"), (low(g_latent), "xy"),
            (low(vectors), "yx"),
        ]
        (
            r_up_enc, r_out_enc, r_up_self, r_value_self, r_key_self,
            r_down_enc, r_down_self, r_out_self, r_value_dec, r_key_dec, r_query_self, r_query_enc,
        ), (
            r_dec_query, r_position, r_value_enc, r_out_dec, r_emb, r_key_enc, r_query_dec, r_latent, r_vectors,
        ) = reduce_all((first_side, second_side), others)
    else:
        r_dec_query, r_out_dec, r_value_dec = reducer.reduce([g_dec_query, g_out_dec, tn(n4, dv_d)], order_yx)
        r_down_self, r_up_self, r_out_self = reducer.reduce(
            [tn(h2, dlat16), tn(n3, du2), tn(a_s, das16)], order_xy
        )
        r_value_self, r_down_enc = reducer.reduce([tn(n2, dv_s), tn(h1, denc16)], order_yx)
        r_up_enc, r_out_enc = reducer.reduce([tn(n1, du1), tn(a_e, daft16)], order_xy)
        r_query_dec, r_key_dec, r_query_self, r_key_self = reducer.reduce(
            [g_query_dec, tn(n4, dk_d), tn(n2, dq_s), tn(n2, dk_s)], order_xy
        )
        r_value_enc, r_latent = reducer.reduce([g_value_enc, g_latent], order_xy)
        (r_position,) = reducer.reduce([dbytes], order_yx)
        r_key_enc, r_query_enc = reducer.reduce([g_key_enc, tn(nl, dq_e)], order_yx)
        (r_emb,) = reducer.reduce([g_table], order_yx)
        (r_vectors,) = reducer.reduce([vectors], order_xy)

    plain = [
        r_position, r_key_enc, r_value_enc, r_latent, r_query_enc, r_out_enc, r_up_enc, r_down_enc,
        r_query_self, r_key_self, r_value_self, r_out_self, r_up_self, r_down_self, r_key_dec, r_value_dec,
        r_dec_query, r_query_dec, r_out_dec,
    ]
    plain, r_embedding, (r_mask, r_gain_bytes, r_gain_dec_q, r_gain_final), gains = finish(plain, r_emb, r_vectors, vocab, 1 + len(gains))
    (
        r_position, r_key_enc, r_value_enc, r_latent, r_query_enc, r_out_enc, r_up_enc, r_down_enc,
        r_query_self, r_key_self, r_value_self, r_out_self, r_up_self, r_down_self, r_key_dec, r_value_dec,
        r_dec_query, r_query_dec, r_out_dec,
    ) = plain
    (
        r_gain_latent, r_gain_enc_mlp, r_gain_self, r_gain_self_mlp, r_gain_dec_kv,
    ) = gains
    return (
        logits_out, r_embedding.T, r_position, r_mask, r_gain_bytes, r_key_enc, r_value_enc,
        r_latent, r_gain_latent, r_query_enc, r_out_enc, r_gain_enc_mlp, r_up_enc, r_down_enc, r_gain_self,
        r_query_self, r_key_self, r_value_self, r_out_self, r_gain_self_mlp, r_up_self, r_down_self,
        r_gain_dec_kv, r_key_dec, r_value_dec, r_dec_query, r_gain_dec_q, r_query_dec, r_out_dec, r_gain_final,
    )


def solution(mesh):
    split = P("items", "blk")
    rows = P(("items", "blk"))
    outs = [P("items", "blk", None), P(None, ("items", "blk"))] + [rows] * 28
    return jax.shard_map(
        local,
        mesh=mesh,
        in_specs=(split, P("items", None), P("items", None)) + (P(),) * 29 + (P("items", "blk", None),),
        out_specs=tuple(outs),
        check_vma=False,
    )
```

profile of v0, /device:TPU:0, one launch (start us, length us, event | category | flops | bytes accessed | tf_op | source)
XLA Modules:
  0.0 342.0 jit_solution(10231911680704917589)
XLA Ops:
  0.7 0.0 copy-start.3
  0.7 0.8 broadcast_select_fusion.4
  1.5 3.0 collective-permute-start
  4.5 1.5 copy.76
  6.1 1.0 copy-done.4
  7.1 0.9 select_bitcast_fusion.1.refs_0_
  7.9 0.0 copy-done.21
  8.0 0.0 copy-done.11
  8.0 0.2 convert_reduce_fusion
  8.2 0.0 copy-start.12
  8.2 0.0 copy-start.17
  8.2 0.0 copy-start.13
  8.2 0.0 copy-start.14
  8.2 0.0 copy-start.15
  8.2 0.0 copy-start.16
  8.3 0.0 copy-start.18
  8.3 0.0 copy-start.19
  8.3 0.3 fusion.7
  8.6 0.0 copy-start.8
  8.6 0.1 fusion.17
  8.7 0.3 fusion.9.refs_15_.refs_9_
  9.0 0.3 convolution_convert_fusion.1.refs_12_
  9.4 0.3 convolution_convert_fusion.refs_3_
  9.7 0.0 copy-done.12
  9.7 0.6 broadcast_in_dim.99.refs_6_
  10.4 0.6 broadcast_in_dim.101.refs_17_
  11.0 0.0 copy-done.17
  11.0 0.6 broadcast_in_dim.89.refs_2_
  11.6 0.0 copy-done.14
  11.6 0.6 broadcast_in_dim.90.refs_3_
  12.2 0.6 broadcast_in_dim.91.refs_4_
  12.8 0.6 broadcast_in_dim.92.refs_5_
  13.4 0.6 broadcast_in_dim.93.refs_7_
  14.0 0.6 broadcast_in_dim.94.refs_8_
  14.6 0.8 copy.73.refs_16_
  15.4 0.8 pad.9.refs_2_
  16.2 0.1 pad.14.clone
  16.3 0.0 collective-permute-done
  16.3 0.6 broadcast_select_fusion.5
  16.9 0.0 collective-permute-start.1
  16.9 4.1 %fusion.22 = (f32[2048]{0:T(1024)S(1)}, f32[2048,768]{1,0:T(8,128)S(1)}) fusion(bf16[2048,768]{1,0:T(8,128)(2,1)} %param.37, bf16[1,768]{1,0:T(2,128)(2,1)S(1)} %broadcast_in_dim.87, bf16[262,768]{1,0:T(8,128)(2,1)S(1)} %copy-done.8, bf16[384]{0:T(512)(128)(2,1)S(1)} %pad.14.clone, s32[2048]{0:T(1024)S(1)} %get-tuple-element.232), kind=kOutput, calls=%fused_computation.56 | convolution fusion | flops 1215232000 | bytes 9858304 | tf_op jit(solution)/shard_map/dot_general | solution.py:17
  21.0 0.8 multiply_reduce_fusion
  21.9 3.2 fusion.21
  25.1 2.4 fusion.23
  27.5 5.4 %online-softmax = f32[256,768]{1,0:T(8,128)} custom-call(f32[256,2048]{1,0:T(8,128)} %get-tuple-element.241, f32[2048,768]{1,0:T(8,128)} %get-tuple-element.227), custom_call_target="tpu_custom_call" | custom-call | tf_op online-softmax
  32.9 1.9 convert_element_type.44.refs_1_.refs_11_
  34.8 1.3 copy.72.refs_5_
  36.2 18.5 %shard_map.545 = (bf16[256,1280]{1,0:T(8,128)(2,1)}, bf16[256,1280]{1,0:T(8,128)(2,1)}, f32[256,1280]{1,0:T(8,128)}, bf16[256,1280]{1,0:T(8,128)(2,1)}, bf16[256...) custom-call(bf16[256,1280]{1,0:T(8,128)(2,1)} %refs_0_.2, ...), custom_call_target="tpu_custom_call" | custom-call | tf_op jit(solution)/shard_map/pallas_call | solution.py:775
  54.7 0.4 fusion.3
  55.2 0.6 reshape_select_fusion.refs_7_
  55.8 0.0 collective-permute-done.1
  55.8 0.2 copy-done.5
  56.0 0.1 bitcast_select_fusion.1
  56.1 13.7 %fusion.10.refs_1_ = bf16[272,2048]{1,0:T(8,128)(2,1)} fusion(bf16[262,1024]{1,0:T(8,128)(2,1)S(1)} %get-tuple-element.229, bf16[262,1024]{1,0:T(8,128)(2,1)S(1)} %get-tuple-element.228), kind=kLoop, calls=%fused_computation.22 | loop fusion | flops 3899392 | bytes 2187264 | tf_op jit(solution)/shard_map/concatenate | solution.py:926
  69.8 24.6 %shard_map.546 = (bf16[272,2048]{1,0:T(8,128)(2,1)}, bf16[2048,768]{1,0:T(8,128)(2,1)}, f32[272,768]{1,0:T(8,128)}, f32[8,768]{1,0:T(8,128)}, bf16[256,256]{1,0:...) custom-call(bf16[2048,768]{1,0:T(8,128)(2,1)} %refs_0_.3, ...), custom_call_target="tpu_custom_call" | custom-call | tf_op jit(solution)/shard_map/pallas_call | solution.py:592
  94.4 1.3 select_bitcast_fusion
  95.7 2.1 collective-permute-start.2
  97.8 2.1 fusion.19
  99.9 25.8 %shard_map.547 = (bf16[256,1280]{1,0:T(8,128)(2,1)}, bf16[256,1280]{1,0:T(8,128)(2,1)}, bf16[256,1280]{1,0:T(8,128)(2,1)}, bf16[256,256]{1,0:T(8,128)(2,1)}, bf1...) custom-call(bf16[256,256]{1,0:T(8,128)(2,1)} %get-tuple-element.138., ...), custom_call_target="tpu_custom_call" | custom-call | tf_op jit(solution)/shard_map/pallas_call | solution.py:775
  125.8 19.7 %shard_map.548 = (bf16[2048,768]{1,0:T(8,128)(2,1)}, bf16[768,384]{1,0:T(8,128)(2,1)}, bf16[1280,128]{1,0:T(8,128)(2,1)}, bf16[256,256]{1,0:T(8,128)(2,1)}, bf16...) custom-call(bf16[256,2048]{1,0:T(8,128)(2,1)} %get-tuple-element.224.refs_0_, ...), custom_call_target="tpu_custom_call" | custom-call | tf_op jit(solution)/shard_map/pallas_call | solution.py:680
  145.5 189.4 %shard_map.549 = (f32[40,1280]{1,0:T(8,128)}, f32[40,1280]{1,0:T(8,128)}, f32[40,1280]{1,0:T(8,128)}, f32[40,1280]{1,0:T(8,128)}, f32[40,256]{1,0:T(8,128)}, /*i...) custom-call(bf16[256,1280]{1,0:T(8,128)(2,1)} %get-tuple-element.130, ...), custom_call_target="tpu_custom_call" | custom-call | tf_op jit(solution)/shard_map/pallas_call | solution.py:463
  334.9 4.3 %shard_map.550 = (f32[64,768]{1,0:T(8,128)}, f32[24,256]{1,0:T(8,128)}, f32[24,1280]{1,0:T(8,128)}, f32[8,1280]{1,0:T(8,128)}, f32[40,256]{1,0:T(8,128)}, /*inde...) custom-call(f32[64,768]{1,0:T(8,128)} %get-tuple-element.174.refs_0_, ...), custom_call_target="tpu_custom_call" | custom-call | tf_op jit(solution)/shard_map/pallas_call | solution.py:511
  339.1 0.0 collective-permute-done.2
  339.2 2.4 broadcast_select_fusion
  (40 shorter events, 0.1 us)
Async XLA Ops:
  0.7 7.3 %copy-start.21 = (s32[2,8]{1,0:T(2,128)S(1)}, s32[2,8]{1,0:T(2,128)}, u32[]{:S(2)}) copy-start(s32[2,8]{1,0:T(2,128)} %param.34) | copy-start | bytes 196
  0.7 7.3 %copy-start.20 = (s32[2,8]{1,0:T(2,128)S(1)}, s32[2,8]{1,0:T(2,128)}, u32[]{:S(2)}) copy-start(s32[2,8]{1,0:T(2,128)} %param.35) | copy-start | bytes 196
  0.7 7.3 %copy-start.11 = (bf16[1280]{0:T(1024)(128)(2,1)S(1)}, bf16[1280]{0:T(1024)(128)(2,1)}, u32[]{:S(2)}) copy-start(bf16[1280]{0:T(1024)(128)(2,1)} %param.43) | copy-start | bytes 7684
  0.7 7.3 %copy-start.3 = (bf16[256,1280]{1,0:T(8,128)(2,1)S(1)}, bf16[256,1280]{1,0:T(8,128)(2,1)}, u32[]{:S(2)}) copy-start(bf16[256,1280]{1,0:T(8,128)(2,1)} %refs_0_.2) | copy-start | bytes 1966084
  1.5 14.8 %collective-permute-start = (s32[1024]{0:T(1024)S(1)}, s32[1024]{0:T(1024)S(1)}, u32[]{:S(2)}, u32[]{:S(2)}) collective-permute-start(s32[1024]{0:T(1024)S(1)} %bitcast.56), channel_id=1, source_target_pairs={{0,1},{1,0},{2,3},{3,2},{4,5},{5,4},{6,7},{7,6},{8,9},{9,8},{10,11... | collective-permute-start | bytes 12296 | tf_op jit(solution)/shard_map/ppermute | solution.py:916
  6.1 1.0 copy-start.4
  7.1 1.9 copy-start.7
  7.9 1.4 copy-start.9
  8.2 1.5 copy-start.12
  8.2 2.8 copy-start.17
  8.2 2.8 copy-start.13
  8.2 3.4 copy-start.14
  8.2 4.0 %copy-start.15 = (bf16[1280]{0:T(1024)(128)(2,1)S(1)}, bf16[1280]{0:T(1024)(128)(2,1)}, u32[]{:S(2)}) copy-start(bf16[1280]{0:T(1024)(128)(2,1)} %param.54) | copy-start | bytes 7684
  8.2 4.6 %copy-start.16 = (bf16[1280]{0:T(1024)(128)(2,1)S(1)}, bf16[1280]{0:T(1024)(128)(2,1)}, u32[]{:S(2)}) copy-start(bf16[1280]{0:T(1024)(128)(2,1)} %param.57) | copy-start | bytes 7684
  8.3 5.2 %copy-start.18 = (bf16[768]{0:T(1024)(128)(2,1)S(1)}, bf16[768]{0:T(1024)(128)(2,1)}, u32[]{:S(2)}) copy-start(bf16[768]{0:T(1024)(128)(2,1)} %param.61) | copy-start | bytes 4612
  8.3 5.7 %copy-start.19 = (bf16[768]{0:T(1024)(128)(2,1)S(1)}, bf16[768]{0:T(1024)(128)(2,1)}, u32[]{:S(2)}) copy-start(bf16[768]{0:T(1024)(128)(2,1)} %param.64) | copy-start | bytes 4612
  8.6 6.8 %copy-start.8 = (bf16[262,768]{1,0:T(8,128)(2,1)S(1)}, bf16[262,768]{1,0:T(8,128)(2,1)}, u32[]{:S(2)}) copy-start(bf16[262,768]{1,0:T(8,128)(2,1)} %param.36) | copy-start | bytes 1207300
  9.0 7.9 %copy-start.2 = (bf16[256,1280]{1,0:T(8,128)(2,1)}, bf16[256,1280]{1,0:T(8,128)(2,1)S(1)}, u32[]{:S(2)}) copy-start(bf16[256,1280]{1,0:T(8,128)(2,1)S(1)} %fusion.9.refs_15_.refs_9_) | copy-start | bytes 1966084
  9.4 11.6 %copy-start.10 = (bf16[256,256]{1,0:T(8,128)(2,1)}, bf16[256,256]{1,0:T(8,128)(2,1)S(1)}, u32[]{:S(2)}) copy-start(bf16[256,256]{1,0:T(8,128)(2,1)S(1)} %convolution_convert_fusion.1.refs_12_) | copy-start | bytes 393220
  9.7 15.4 %copy-start.6 = (bf16[256,768]{1,0:T(8,128)(2,1)}, bf16[256,768]{1,0:T(8,128)(2,1)S(1)}, u32[]{:S(2)}) copy-start(bf16[256,768]{1,0:T(8,128)(2,1)S(1)} %convolution_convert_fusion.refs_3_) | copy-start | bytes 1179652
  16.9 38.9 %collective-permute-start.1 = (bf16[262,1024]{1,0:T(8,128)(2,1)}, bf16[262,1024]{1,0:T(8,128)(2,1)S(1)}, u32[]{:S(2)}, u32[]{:S(2)}) collective-permute-start(bf16[262,1024]{1,0:T(8,128)(2,1)} %shard_map.544), channel_id=1, source_target_pairs={{0,1},{1,0},{2,3},{3,2},{4,5},{5,4},{6,7},{7,6},{8,9},{9,8},{10,11... | collective-permute-start | bytes 1609736 | tf_op jit(solution)/shard_map/ppermute | solution.py:916
  25.1 2.4 copy-start.1
  36.2 18.6 %copy-start = (f32[256,2048]{1,0:T(8,128)S(1)}, f32[256,2048]{1,0:T(8,128)}, u32[]{:S(2)}) copy-start(f32[256,2048]{1,0:T(8,128)} %get-tuple-element.241) | copy-start | bytes 6291460
  54.7 1.2 copy-start.5
  95.7 243.4 %collective-permute-start.2 = (bf16[262,1024]{1,0:T(8,128)(2,1)S(1)}, bf16[262,1024]{1,0:T(8,128)(2,1)S(1)}, u32[]{:S(2)}, u32[]{:S(2)}) collective-permute-start(bf16[262,1024]{1,0:T(8,128)(2,1)S(1)} %get-tuple-element.231), channel_id=1, source_target_pairs={{0,1},{1,0},{2,3},{3,2},{4,5},{5,4},{6,7},{7,6},{8,9},{9,8},{10,11... | collective-permute-start | bytes 1609736 | tf_op jit(solution)/shard_map/ppermute | solution.py:916
where the time goes:
time: 348 us; the launch traced here: 342 us
  Pallas kernels  288 us (83%)
  other arithmetic  29.8 us (9%)
  local copies, waits for them, and re-layouts  10.6 us (3%)
  matrix products  7.14 us (2%)
  starting transfers between devices  5.12 us (1%)
    pallas_call x1, Pallas kernels, reduce_all(): pl.pallas_call(lambda *refs: reduce_kernel(plan, *refs), out_shape=[jax.S...  189 us
    pallas_call x2, Pallas kernels, streamed(): pl.pallas_call(kernel, out_shape=shapes, in_specs=[pl.BlockSpec(memory_sp...  44.4 us
    pallas_call x1, Pallas kernels, decoder_pass(): pl.pallas_call(lambda *refs: decoder_kernel(scale, *refs), grid=(rows //...  24.6 us
    pallas_call x1, Pallas kernels, bytes_backward(): pl.pallas_call(lambda *refs: bytes_kernel(at, scale, *refs), grid=(rows /...  19.7 us
    concatenate x1, other arithmetic, own_item(): return jnp.concatenate([low_half, high_half], axis=-1)  13.7 us
  transfers between devices with their start and end apart: 3, of which 0 were waited for; matrix products, arithmetic and copies ran while one was open for 8% of the time, Pallas kernels for 77%

commit v1 on v0

--- a/solution.py
+++ b/solution.py
@@ -530,84 +530,6 @@
     return rstd * (dhat - first - hat * second)
 
 
-def decoder_kernel(
-    scale, query, cot, emb, key, value, w_query, w_out, gain_q, gain_f,
-    logits, dquery, g_emb, g_gains, dkey, dvalue, g_query, g_out,
-    g_pd, g_dn, kq, vo, vo_mid,
-):
-    @pl.when(pl.program_id(0) == 0)
-    def _():
-        for ref in (g_emb, g_pd, g_dn, g_gains):
-            ref[...] = jnp.zeros_like(ref)
-        kq[...] = nt(key[...], w_query[...]).astype(BF16)
-        out = nn(value[...], w_out[...])
-        vo[...] = out.astype(BF16)
-        vo_mid[...] = (out - jnp.mean(out, axis=0, keepdims=True)).astype(BF16)
-
-    x = query[...].astype(F32)
-    hat_q, rstd_q = center(x)
-    gq, gf = gain_q[...].astype(F32), gain_f[...].astype(F32)
-    nq = (hat_q * gq).astype(BF16)
-    soft = softmax(nt(nq, kq[...]) * scale)
-    p = soft.astype(BF16)
-    hat_f, rstd_f = center(x + nn(p, vo[...]))
-    nf = (hat_f * gf).astype(BF16)
-    logits[...] = nt(emb[...], nf).astype(BF16)
-    dnf = nn(cot[...].T, emb[...])
-    g_emb[...] += nn(cot[...], nf)
-    g_gains[0:1] += jnp.sum(dnf * hat_f, axis=0, keepdims=True)
-    ddec = center_backward(dnf * gf, hat_f, rstd_f)
-    ddec16 = ddec.astype(BF16)
-    g_pd[...] += nn(p.T, ddec16)
-    ds = softmax_backward(nt(ddec16, vo_mid[...]), soft, scale)
-    g_dn[...] += nn(ds.T, nq)
-    dnq = nn(ds, kq[...])
-    g_gains[1:2] += jnp.sum(dnq * hat_q, axis=0, keepdims=True)
-    dquery[...] = (ddec + center_backward(dnq * gq, hat_q, rstd_q)).astype(BF16)
-
-    @pl.when(pl.program_id(0) == pl.num_programs(0) - 1)
-    def _():
-        pd, dn = g_pd[...].astype(BF16), g_dn[...].astype(BF16)
-        dvalue[...] = nt(pd, w_out[...]).astype(BF16)
-        dkey[...] = nn(dn, w_query[...]).astype(BF16)
-        g_out[...] = nn(value[...].T, pd).astype(BF16)
-        g_query[...] = nn(dn.T, key[...]).astype(BF16)
-
-
-def decoder_pass(query, cot, emb, key, value, w_query, w_out, gain_q, gain_f, scale):
-    rows, width = query.shape
-    vocab, latents, block = emb.shape[0], key.shape[0], 512
-
-    def whole(x):
-        return pl.BlockSpec(x.shape, lambda i: (0, 0))
-
-    sums = jax.ShapeDtypeStruct((latents, width), F32)
-    shapes = [
-        jax.ShapeDtypeStruct((vocab, rows), BF16),
-        jax.ShapeDtypeStruct((rows, width), BF16),
-        jax.ShapeDtypeStruct((vocab, width), F32),
-        jax.ShapeDtypeStruct((8, width), F32),
-    ] + [jax.ShapeDtypeStruct(x.shape, BF16) for x in (key, value, w_query, w_out)]
-    small = (gain_q[None, :], gain_f[None, :])
-    return pl.pallas_call(
-        lambda *refs: decoder_kernel(scale, *refs),
-        grid=(rows // block,),
-        out_shape=shapes,
-        in_specs=[
-            pl.BlockSpec((block, width), lambda i: (i, 0)),
-            pl.BlockSpec((vocab, block), lambda i: (0, i)),
-        ]
-        + [whole(x) for x in (emb, key, value, w_query, w_out) + small],
-        out_specs=[
-            pl.BlockSpec((vocab, block), lambda i: (0, i)),
-            pl.BlockSpec((block, width), lambda i: (i, 0)),
-        ]
-        + [whole(x) for x in shapes[2:]],
-        scratch_shapes=[pltpu.VMEM(sums.shape, F32)] * 2 + [pltpu.VMEM(sums.shape, BF16)] * 3,
-        compiler_params=pltpu.CompilerParams(vmem_limit_bytes=56 * 1024 * 1024),
-    )(query, cot, emb, key, value, w_query, w_out, *small)
-
-
 def bytes_kernel(
     at, scale, p, soft, vd, qk, nb, rstd, gain, codes, emb, sums, wide,
     pn, q, dae, daft, nl, rstd_l, gain_l, w_key, w_query,
@@ -743,29 +665,41 @@
 
 class Results:
     def __init__(self, stage, targets, sem):
-        self.stage, self.targets, self.sem, self.copies = stage, targets, sem, []
-
-    def put(self, value):
+        self.stage, self.targets, self.sem, self.copies, self.left = stage, targets, sem, [], set()
+
+    def put(self, value, over=None):
         i = len(self.copies)
-        self.stage[i][...] = value.astype(self.stage[i].dtype)
-        copy = pltpu.make_async_copy(self.stage[i], self.targets[i], self.sem.at[i])
+        buffer = self.stage[i if over is None else over]
+        if over is not None:
+            self.copies[over].wait()
+            self.left.add(over)
+        buffer[...] = value.astype(buffer.dtype)
+        copy = pltpu.make_async_copy(buffer, self.targets[i], self.sem.at[i])
         copy.start()
         self.copies.append(copy)
-        return self.stage[i]
+        return buffer
+
+    def send(self, source):
+        i = len(self.copies)
+        copy = pltpu.make_async_copy(source, self.targets[i], self.sem.at[i])
+        copy.start()
+        self.copies.append(copy)
 
     def finish(self):
-        for copy in self.copies:
-            copy.wait()
-
-
-def streamed(body, small, large, shapes, extra):
+        for i, copy in enumerate(self.copies):
+            if i not in self.left:
+                copy.wait()
+
+
+def streamed(body, small, large, shapes, extra, unstaged):
     n_s, n_l, n_o = len(small), len(large), len(shapes)
 
     def kernel(*refs):
         ins, refs = refs[: n_s + n_l], refs[n_s + n_l :]
         outs, refs = refs[:n_o], refs[n_o:]
         held, refs = refs[:n_l], refs[n_l:]
-        stage, refs = refs[:n_o], refs[n_o:]
+        kept, refs = list(refs[: n_o - len(unstaged)]), refs[n_o - len(unstaged) :]
+        stage = [None if i in unstaged else kept.pop(0) for i in range(n_o)]
         stream = Stream(ins[n_s:], held, refs[0])
         results = Results(stage, outs, refs[1])
         body(ins[:n_s], stream, results, refs[2:])
@@ -778,24 +712,23 @@
         in_specs=[pl.BlockSpec(memory_space=pltpu.VMEM)] * n_s + [anywhere] * n_l,
         out_specs=[anywhere] * n_o,
         scratch_shapes=[pltpu.VMEM(x.shape, x.dtype) for x in large]
-        + [pltpu.VMEM(x.shape, x.dtype) for x in shapes]
+        + [pltpu.VMEM(x.shape, x.dtype) for i, x in enumerate(shapes) if i not in unstaged]
         + [pltpu.SemaphoreType.DMA((n_l,)), pltpu.SemaphoreType.DMA((n_o,))]
         + extra,
-        compiler_params=pltpu.CompilerParams(vmem_limit_bytes=60 * 1024 * 1024),
+        compiler_params=pltpu.CompilerParams(vmem_limit_bytes=63 * 1024 * 1024),
     )(*small, *large)
 
 
-def spread(column):
-    return jnp.broadcast_to(column, (column.shape[0], 128))
-
-
-def latent_forward(latent, pn, gains, weights):
+def middle_pass(latent, pn, gains, byte_gains, weights, scale):
     rows, width = latent.shape
-    wide, narrow = (rows, width), (rows, weights[4].shape[1])
+    emb, queries, cot = weights[14:]
+    entries, depth = emb.shape
+    block = 256
+    qk = weights[4].shape[1]
 
     def body(small, w, results, extra):
-        latent_ref, pn_ref, g1, g2, g3, g4 = small
-        (total,) = extra
+        latent_ref, pn_ref, g1, g2, g3, g4, gain_q, gain_f = small
+        total, dq_sum, dk_sum, sums, u1, u2, q, k, v, k_d, v_d, kq, vo, vo_mid, g_pd, g_dn, g_emb, g_byte = extra
         put = results.put
 
         def norm(x, gain):
@@ -805,95 +738,121 @@
         a_e = put(nn(pn_ref[...], w[0]))
         x = latent_ref[...].astype(F32) + nn(a_e[...], w[1])
         n1, r1 = norm(x, g1)
-        u1 = put(nn(n1[...], w[2]))
+        u1[...] = nn(n1[...], w[2])
         h1 = put(gelu_forward(u1[...]))
         x = x + nn(h1[...], w[3])
         n2, r2 = norm(x, g2)
-        q, k, v = put(nn(n2[...], w[4])), put(nn(n2[...], w[5])), put(nn(n2[...], w[6]))
+        q[...] = nn(n2[...], w[4]).astype(BF16)
+        k[...] = nn(n2[...], w[5]).astype(BF16)
+        v[...] = nn(n2[...], w[6]).astype(BF16)
         self_forward_heads(q, k, v, total)
         a_s = put(total[...])
         x = x + nn(a_s[...], w[7])
         n3, r3 = norm(x, g3)
-        u2 = put(nn(n3[...], w[8]))
+        u2[...] = nn(n3[...], w[8])
         h2 = put(gelu_forward(u2[...]))
         x = x + nn(h2[...], w[9])
         n4, r4 = norm(x, g4)
-        put(nn(n4[...], w[10]))
-        put(nn(n4[...], w[11]))
-        for r in (r1, r2, r3, r4):
-            put(spread(r))
-
-    def low(shape):
+        k_d[...] = nn(n4[...], w[10]).astype(BF16)
+        v_d[...] = nn(n4[...], w[11]).astype(BF16)
+
+        w_query, w_out = w[12], w[13]
+        kq[...] = nt(k_d[...], w_query).astype(BF16)
+        out = nn(v_d[...], w_out)
+        vo[...] = out.astype(BF16)
+        vo_mid[...] = (out - jnp.mean(out, axis=0, keepdims=True)).astype(BF16)
+        for ref in (g_pd, g_dn, g_emb, g_byte):
+            ref[...] = jnp.zeros_like(ref)
+        w[14], w[15], w[16]
+        emb_ref, query_ref, cot_ref = w.targets[14:]
+
+        def decode(i, carry):
+            at = pl.ds(pl.multiple_of(i * block, block), block)
+            x = query_ref[at, :].astype(F32)
+            hat_q, rstd_q = center(x)
+            gq, gf = gain_q[...].astype(F32), gain_f[...].astype(F32)
+            nq = (hat_q * gq).astype(BF16)
+            soft = softmax(nt(nq, kq[...]) * scale)
+            p = soft.astype(BF16)
+            hat_f, rstd_f = center(x + nn(p, vo[...]))
+            nf = (hat_f * gf).astype(BF16)
+            cot_part = cot_ref[:, at]
+            dnf = nn(cot_part.T, emb_ref[...])
+            g_emb[...] += nn(cot_part, nf)
+            cot_ref[:, at] = nt(emb_ref[...], nf).astype(BF16)
+            g_byte[0:1] += jnp.sum(dnf * hat_f, axis=0, keepdims=True)
+            ddec = center_backward(dnf * gf, hat_f, rstd_f)
+            ddec16 = ddec.astype(BF16)
+            g_pd[...] += nn(p.T, ddec16)
+            ds = softmax_backward(nt(ddec16, vo_mid[...]), soft, scale)
+            g_dn[...] += nn(ds.T, nq)
+            dnq = nn(ds, kq[...])
+            g_byte[1:2] += jnp.sum(dnq * hat_q, axis=0, keepdims=True)
+            query_ref[at, :] = (ddec + center_backward(dnq * gq, hat_q, rstd_q)).astype(BF16)
+            return carry
+
+        lax.fori_loop(0, queries.shape[0] // block, decode, 0)
+        results.send(query_ref)
+        results.send(cot_ref)
+        results.send(g_emb)
+        results.send(g_byte)
+        pd, dn = g_pd[...].astype(BF16), g_dn[...].astype(BF16)
+        dk_d = nn(dn, w.targets[12][...]).astype(BF16)
+        dv_d = nt(pd, w.targets[13][...]).astype(BF16)
+        put(dk_d)
+        put(dv_d)
+        put(nn(dn.T, k_d[...]))
+        put(nn(v_d[...].T, pd))
+
+        sums[...] = jnp.zeros_like(sums)
+
+        def back(dy, normed, rstd, gain, row):
+            g = gain[...].astype(F32)
+            hat = normed[...].astype(F32) / g
+            sums[row : row + 1] = jnp.sum(dy * hat, axis=0, keepdims=True)
+            return center_backward(dy * g, hat, rstd)
+
+        dlat = back(nt(dk_d, w[10]) + nt(dv_d, w[11]), n4, r4, g4, 4)
+        dlat16 = put(dlat, 0)
+        du2 = put(gelu_backward(nt(dlat16[...], w[9]), u2[...]), 2)
+        das = dlat + back(nt(du2[...], w[8]), n3, r3, g3, 3)
+        das16 = put(das, 4)
+        da = nt(das16[...], w[7]).astype(BF16)
+        self_backward_heads(q, k, v, da, dq_sum, dk_sum, total)
+        dq, dk, dv = put(dq_sum[...]), put(dk_sum[...]), put(total[...], 6)
+        dn2 = nt(dq[...], w[4]) + nt(dk[...], w[5]) + nt(dv[...], w[6])
+        denc = das + back(dn2, n2, r2, g2, 2)
+        denc16 = put(denc, 7)
+        du1 = put(gelu_backward(nt(denc16[...], w[3]), u1[...]), 5)
+        daft = denc + back(nt(du1[...], w[2]), n1, r1, g1, 1)
+        daft16 = put(daft, 3)
+        u1[...] = daft
+        results.send(u1)
+        dae = put(nt(daft16[...], w[1]), 1)
+        put(nt(dae[...], w[0]))
+        results.send(sums)
+
+    wide = (rows, width)
+
+    def low(*shape):
         return jax.ShapeDtypeStruct(shape, BF16)
 
-    full = jax.ShapeDtypeStruct(wide, F32)
-    shapes = [low(wide), low(wide), full, low(wide), low(wide), low(narrow), low(narrow), low(wide)]
-    shapes += [low(wide), low(wide), full, low(wide), low(wide)]
-    shapes += [low((rows, weights[10].shape[1])), low((rows, weights[11].shape[1]))]
-    shapes += [jax.ShapeDtypeStruct((rows, 128), F32)] * 4
-    small = [latent, pn] + [g[None, :] for g in gains]
-    return streamed(body, small, weights, shapes, [pltpu.VMEM(wide, F32)])
-
-
-def latent_backward(dk_d, dv_d, gains, kept, weights):
-    rows, width = kept[0].shape
-    count = len(weights)
-
-    def body(small, stream, results, extra):
-        dk_ref, dv_ref, g1, g2, g3, g4 = small
-        dq_sum, dk_sum, dv_sum, sums = extra
-        put = results.put
-        w = stream
-        sums[...] = jnp.zeros_like(sums)
-
-        def norm(dy, normed, rstd, gain, row):
-            g = gain[...].astype(F32)
-            hat = normed.astype(F32) / g
-            sums[row : row + 1] = jnp.sum(dy * hat, axis=0, keepdims=True)
-            return center_backward(dy * g, hat, rstd[:, :1])
-
-        n4, u2, n3, q, k, v, n2, u1, n1, r4, r3, r2, r1 = range(count, count + 13)
-        dlat = norm(nt(dk_ref[...], w[0]) + nt(dv_ref[...], w[1]), w[n4], w[r4], g4, 4)
-        dlat16 = put(dlat)
-        du2 = put(gelu_backward(nt(dlat16[...], w[2]), w[u2]))
-        das = dlat + norm(nt(du2[...], w[3]), w[n3], w[r3], g3, 3)
-        das16 = put(das)
-        da = nt(das16[...], w[4]).astype(BF16)
-        w[q], w[k], w[v]
-        self_backward_heads(w.targets[q], w.targets[k], w.targets[v], da, dq_sum, dk_sum, dv_sum)
-        dq, dk, dv = put(dq_sum[...]), put(dk_sum[...]), put(dv_sum[...])
-        dn2 = nt(dq[...], w[5]) + nt(dk[...], w[6]) + nt(dv[...], w[7])
-        denc = das + norm(dn2, w[n2], w[r2], g2, 2)
-        denc16 = put(denc)
-        du1 = put(gelu_backward(nt(denc16[...], w[8]), w[u1]))
-        daft = denc + norm(nt(du1[...], w[9]), w[n1], w[r1], g1, 1)
-        daft16 = put(daft)
-        put(daft)
-        dae = put(nt(daft16[...], w[10]))
-        put(nt(dae[...], w[11]))
-        put(sums[...])
-
-    wide = (rows, width)
-    low, narrow = jax.ShapeDtypeStruct(wide, BF16), jax.ShapeDtypeStruct(kept[3].shape, BF16)
-    shapes = [low, low, low, narrow, narrow, low, low, low, low, jax.ShapeDtypeStruct(wide, F32), low]
-    shapes += [jax.ShapeDtypeStruct((rows, weights[11].shape[0]), BF16), jax.ShapeDtypeStruct((8, width), F32)]
-    extra = [pltpu.VMEM(x.shape, F32) for x in kept[3:6]] + [pltpu.VMEM((8, width), F32)]
-    large = list(weights) + list(kept)
-    order = [0, 1, count, count + 9, 2, count + 1, 3, count + 2, count + 10, 4, count + 3, count + 4, count + 5]
-    order += [5, 6, 7, count + 6, count + 11, 8, count + 7, 9, count + 8, count + 12, 10, 11]
-    place = {old: new for new, old in enumerate(order)}
-
-    class Ordered:
-        def __init__(self, stream):
-            self.stream, self.targets = stream, {old: stream.targets[new] for old, new in place.items()}
-
-        def __getitem__(self, i):
-            return self.stream[place[i]]
-
-    small = [dk_d, dv_d] + [g[None, :] for g in gains]
-    return streamed(
-        lambda a, b, c, d: body(a, Ordered(b), c, d), small, [large[i] for i in order], shapes, extra
-    )
+    def full(*shape):
+        return jax.ShapeDtypeStruct(shape, F32)
+
+    shapes = [low(*wide)] * 8
+    shapes += [low(*queries.shape), low(*cot.shape), full(entries, depth), full(8, depth)]
+    shapes += [low(rows, qk), low(rows, depth), low(depth, qk), low(depth, depth)]
+    shapes += [low(*wide)] * 3 + [low(rows, qk)] * 2 + [low(*wide)] * 4
+    shapes += [full(*wide), low(*wide), low(rows, depth), full(8, width)]
+    unstaged = {8, 9, 10, 11, 16, 17, 18, 21, 22, 23, 24, 25, 26, 28}
+    vmem = pltpu.VMEM
+    extra = [vmem(wide, F32), vmem((rows, qk), F32), vmem((rows, qk), F32), vmem((8, width), F32)]
+    extra += [vmem(wide, F32)] * 2 + [vmem((rows, qk), BF16)] * 2 + [vmem(wide, BF16)]
+    extra += [vmem((rows, qk), BF16)] + [vmem((rows, depth), BF16)] * 4 + [vmem((rows, depth), F32)] * 2
+    extra += [vmem((entries, depth), F32), vmem((8, depth), F32)]
+    small = [latent, pn] + [g[None, :] for g in gains + byte_gains]
+    return streamed(body, small, weights, shapes, extra, unstaged)
 
 
 def local(
@@ -955,32 +914,22 @@
     pn_e = nn(p_e, nb).astype(BF16)
     gains = (gain_enc_mlp, gain_self, gain_self_mlp, gain_dec_kv)
     (
-        a_e, n1, u1, h1, n2, q_s, k_s, v_s, a_s, n3, u2, h2, n4, k_d, v_d, rstd1, rstd2, rstd3, rstd4,
-    ) = latent_forward(
-        latent_init, pn_e, gains,
+        a_e, n1, h1, n2, a_s, n3, h2, n4,
+        g_dec_query, logits, g_emb_out, gain_sums, dk_d, dv_d, g_query_dec, g_out_dec,
+        dlat16, du2, das16, dq_s, dk_s, dv_s, denc16, du1, daft16, dafter, dae16, vd_e, wide,
+    ) = middle_pass(
+        latent_init, pn_e, gains, (gain_dec_q, gain_final),
         [
             value_enc, out_enc, up_enc, down_enc, query_self, key_self, value_self, out_self, up_self,
-            down_self, key_dec, value_dec,
+            down_self, key_dec, value_dec, query_dec, out_dec, emb_rows, dec_query, cot,
         ],
-    )
-
-    scale_d = k_d.shape[1] ** (-0.5)
-    logits, g_dec_query, g_emb_out, gain_sums, dk_d, dv_d, g_query_dec, g_out_dec = decoder_pass(
-        dec_query, cot, emb_rows, k_d, v_d, query_dec, out_dec, gain_dec_q, gain_final, scale_d
+        query_dec.shape[1] ** (-0.5),
     )
     logits = logits[:vocab]
     logits_got = swap(jnp.where(me == 0, logits[:, half:], logits[:, :half]))
     logits_own = jnp.where(me == 0, logits[:, :half], logits[:, half:])
     side = lax.broadcasted_iota(jnp.int32, (1, 2, 1), 1)
     logits_out = jnp.where(side == me, logits_own[:, None, :], logits_got[:, None, :]).transpose(1, 2, 0)
-
-    dlat16, du2, das16, dq_s, dk_s, dv_s, denc16, du1, daft16, dafter, dae16, vd_e, wide = latent_backward(
-        dk_d, dv_d, gains, [n4, u2, n3, q_s, k_s, v_s, n2, u1, n1, rstd4, rstd3, rstd2, rstd1],
-        [
-            key_dec, value_dec, down_self, up_self, out_self, query_self, key_self, value_self, down_enc,
-            up_enc, out_enc, value_enc,
-        ],
-    )
 
     dbytes, g_table, vectors, dq_e, g_key_enc, g_value_enc, g_latent = bytes_backward(
         vocab + 1, scale_e, p_e, soft_e, vd_e, qk_e, nb, rstd_b, gain_bytes, codes, g_emb_out, gain_sums, wide,

time: 348 us -> 331 us (0.951)
  Pallas kernels: 288 us -> 277 us
  other arithmetic: 29.8 us -> 24 us
    pallas_call x1 -> x0, Pallas kernels: 24.6 us -> none  [decoder_pass(): pl.pallas_call(lambda *refs: decoder_kernel(scale, *refs), grid=(rows //...]
    pallas_call x2 -> x1, Pallas kernels: 44.4 us -> 58.9 us  [streamed(): pl.pallas_call(kernel, out_shape=shapes, in_specs=[pl.BlockSpec(memory_sp...]
    concatenate x1 -> x2, other arithmetic: 13.7 us -> 1.7 us  [own_item(): return jnp.concatenate([low_half, high_half], axis=-1)]
  transfers between devices with their start and end apart: 3 -> 3, of which waited for: 0 -> 0; matrix products, arithmetic and copies ran while one was open for 8% -> 8% of each run, Pallas kernels for 77% -> 67%
where the time goes in v1:
time: 331 us; the launch traced here: 326 us
  Pallas kernels  277 us (84%)
  other arithmetic  24 us (7%)
  local copies, waits for them, and re-layouts  10.7 us (3%)
  matrix products  7.1 us (2%)
  starting transfers between devices  5.11 us (2%)
    pallas_call x1, Pallas kernels, reduce_all(): pl.pallas_call(lambda *refs: reduce_kernel(plan, *refs), out_shape=[jax.S...  189 us
    pallas_call x1, Pallas kernels, streamed(): pl.pallas_call(kernel, out_shape=shapes, in_specs=[pl.BlockSpec(memory_sp...  58.9 us
    pallas_call x1, Pallas kernels, bytes_backward(): pl.pallas_call(lambda *refs: bytes_kernel(at, scale, *refs), grid=(rows /...  19.7 us
  transfers between devices with their start and end apart: 3, of which 0 were waited for; matrix products, arithmetic and copies ran while one was open for 8% of the time, Pallas kernels for 67%

profile of v1, /device:TPU:0, one launch (start us, length us, event | category | flops | bytes accessed | tf_op | source)
XLA Modules:
  0.0 325.5 jit_solution(11187352085519680499)
XLA Ops:
  0.7 0.0 copy-start.13
  0.7 0.8 broadcast_select_fusion.4
  1.5 3.0 collective-permute-start
  4.5 0.7 convert_element_type.36
  5.2 1.3 convert_reduce_fusion
  6.5 0.0 copy-start.5
  6.5 1.5 fusion.7
  8.0 0.7 dynamic-slice_bitcast_fusion
  8.7 0.7 bitcast_add_fusion
  9.4 0.0 copy-done.13
  9.4 0.3 copy.76
  9.7 0.0 copy-start.11
  9.7 0.9 select_bitcast_fusion.1.refs_0_
  10.6 0.0 copy-start.16
  10.6 0.0 copy-start.17
  10.6 0.0 copy-start.18
  10.6 0.0 copy-start.19
  10.6 0.0 copy-start.21
  10.6 0.0 copy-start.22
  10.6 0.0 copy-start.10
  10.7 0.3 fusion.9.refs_15_.refs_9_
  11.0 0.3 convolution_convert_fusion.1.refs_12_
  11.3 0.0 copy-start.12
  11.3 0.3 convolution_convert_fusion.refs_3_
  11.7 0.1 fusion.17
  11.8 0.6 broadcast_in_dim.95.refs_6_
  12.4 0.6 broadcast_in_dim.97.refs_17_
  13.0 0.6 broadcast_in_dim.85.refs_2_
  13.6 0.6 broadcast_in_dim.86.refs_3_
  14.2 0.0 copy-done.18
  14.2 0.6 broadcast_in_dim.87.refs_4_
  14.8 0.6 broadcast_in_dim.88.refs_5_
  15.4 0.6 broadcast_in_dim.89.refs_6_
  16.0 0.6 broadcast_in_dim.90.refs_7_
  16.6 0.8 copy.73.refs_16_
  17.4 0.8 pad.8.refs_22_
  18.2 0.1 pad.16.clone
  18.2 0.0 collective-permute-done
  18.2 0.6 pad_add_fusion
  18.8 4.1 %fusion.22 = (f32[2048]{0:T(1024)S(1)}, f32[2048,768]{1,0:T(8,128)S(1)}) fusion(bf16[2048,768]{1,0:T(8,128)(2,1)} %param.37, bf16[1,768]{1,0:T(2,128)(2,1)S(1)} %broadcast_in_dim.83, bf16[262,768]{1,0:T(8,128)(2,1)S(1)} %copy-done.10, bf16[384]{0:T(512)(128)(2,1)S(1)} %pad.16.clone, s32[2048]{0:T(1024)S(1)} %get-tuple-element.211), kind=kOutput, calls=%fused_computation.56 | convolution fusion | flops 1215232000 | bytes 9858304 | tf_op jit(solution)/shard_map/dot_general | solution.py:17
  23.0 0.0 copy-done.4
  23.0 0.8 multiply_reduce_fusion
  23.9 1.8 copy-done
  25.7 0.0 collective-permute-start.1
  25.7 5.1 %fusion.21 = (bf16[2048,768]{1,0:T(8,128)(2,1)S(1)}, f32[2048,768]{1,0:T(8,128)}) fusion(f32[768]{0:T(1024)S(1)} %convert_element_type.41, f32[2048]{0:T(1024)S(1)} %add_rsqrt_fusion, f32[2048,768]{1,0:T(8,128)} %copy-done, f32[2048]{0:T(1024)S(1)} %broadcast_multiply_fusion), kind=kLoop, calls=%fused_computation.55 | loop fusion | flops 6291456 | bytes 15748096 | tf_op jit(solution)/shard_map/convert_element_type | solution.py:33
  30.8 2.3 fusion.23
  33.1 5.3 %online-softmax = f32[256,768]{1,0:T(8,128)} custom-call(f32[256,2048]{1,0:T(8,128)} %get-tuple-element.219, f32[2048,768]{1,0:T(8,128)} %get-tuple-element.205), custom_call_target="tpu_custom_call" | custom-call | tf_op online-softmax
  38.5 2.1 convert_element_type.44.refs_1_.refs_11_
  40.6 1.4 copy.72.refs_5_
  41.9 0.4 fusion.3
  42.4 0.6 reshape_select_fusion.refs_7_
  43.0 0.0 collective-permute-done.1
  43.0 0.0 copy-done.7
  43.0 1.1 bitcast_select_fusion.1
  44.1 1.1 fusion.10.refs_24_
  45.2 58.9 %shard_map.545 = (bf16[256,1280]{1,0:T(8,128)(2,1)}, bf16[256,1280]{1,0:T(8,128)(2,1)}, bf16[256,1280]{1,0:T(8,128)(2,1)}, bf16[256,1280]{1,0:T(8,128)(2,1)}, bf...) custom-call(bf16[256,1280]{1,0:T(8,128)(2,1)} %refs_0_.1, ...), custom_call_target="tpu_custom_call" | custom-call | tf_op jit(solution)/shard_map/pallas_call | solution.py:709
  104.1 1.4 select_bitcast_fusion
  105.5 2.1 collective-permute-start.2
  107.6 2.1 fusion.19
  109.7 19.7 %shard_map.546 = (bf16[2048,768]{1,0:T(8,128)(2,1)}, bf16[768,384]{1,0:T(8,128)(2,1)}, bf16[1280,128]{1,0:T(8,128)(2,1)}, bf16[256,256]{1,0:T(8,128)(2,1)}, bf16...) custom-call(bf16[256,2048]{1,0:T(8,128)(2,1)} %get-tuple-element.202.refs_0_, ...), custom_call_target="tpu_custom_call" | custom-call | tf_op jit(solution)/shard_map/pallas_call | solution.py:602
  129.4 189.2 %shard_map.547 = (f32[40,1280]{1,0:T(8,128)}, f32[40,1280]{1,0:T(8,128)}, f32[40,1280]{1,0:T(8,128)}, f32[40,1280]{1,0:T(8,128)}, f32[40,256]{1,0:T(8,128)}, /*i...) custom-call(bf16[256,1280]{1,0:T(8,128)(2,1)} %get-tuple-element.117, ...), custom_call_target="tpu_custom_call" | custom-call | tf_op jit(solution)/shard_map/pallas_call | solution.py:463
  318.6 4.3 %shard_map.548 = (f32[64,768]{1,0:T(8,128)}, f32[24,256]{1,0:T(8,128)}, f32[24,1280]{1,0:T(8,128)}, f32[8,1280]{1,0:T(8,128)}, f32[40,256]{1,0:T(8,128)}, /*inde...) custom-call(f32[64,768]{1,0:T(8,128)} %get-tuple-element.152.refs_0_, ...), custom_call_target="tpu_custom_call" | custom-call | tf_op jit(solution)/shard_map/pallas_call | solution.py:511
  322.9 0.0 collective-permute-done.2
  322.9 2.4 broadcast_select_fusion
  (40 shorter events, 0.1 us)
Async XLA Ops:
  0.7 8.7 %copy-start.13 = (bf16[2,1024,262]{1,0,2:T(2,128)(2,1)S(1)}, bf16[2,1024,262]{1,0,2:T(2,128)(2,1)}, u32[]{:S(2)}) copy-start(bf16[2,1024,262]{1,0,2:T(2,128)(2,1)} %param.65) | copy-start | bytes 3219460
  1.5 16.7 %collective-permute-start = (s32[1024]{0:T(1024)S(1)}, s32[1024]{0:T(1024)S(1)}, u32[]{:S(2)}, u32[]{:S(2)}) collective-permute-start(s32[1024]{0:T(1024)S(1)} %bitcast.56), channel_id=1, source_target_pairs={{0,1},{1,0},{2,3},{3,2},{4,5},{5,4},{6,7},{7,6},{8,9},{9,8},{10,11... | collective-permute-start | bytes 12296 | tf_op jit(solution)/shard_map/ppermute | solution.py:875
  6.5 4.1 %copy-start.5 = (bf16[256,1280]{1,0:T(8,128)(2,1)S(1)}, bf16[256,1280]{1,0:T(8,128)(2,1)}, u32[]{:S(2)}) copy-start(bf16[256,1280]{1,0:T(8,128)(2,1)} %refs_0_.1) | copy-start | bytes 1966084
  9.4 1.6 copy-start.9
  9.7 1.6 copy-start.6
  9.7 1.6 copy-start.11
  10.6 1.2 copy-start.15
  10.6 1.8 copy-start.14
  10.6 2.4 copy-start.20
  10.6 2.4 copy-start.16
  10.6 3.0 copy-start.17
  10.6 3.6 %copy-start.18 = (bf16[1280]{0:T(1024)(128)(2,1)S(1)}, bf16[1280]{0:T(1024)(128)(2,1)}, u32[]{:S(2)}) copy-start(bf16[1280]{0:T(1024)(128)(2,1)} %param.54) | copy-start | bytes 7684
  10.6 4.2 %copy-start.19 = (bf16[1280]{0:T(1024)(128)(2,1)S(1)}, bf16[1280]{0:T(1024)(128)(2,1)}, u32[]{:S(2)}) copy-start(bf16[1280]{0:T(1024)(128)(2,1)} %param.57) | copy-start | bytes 7684
  10.6 4.8 %copy-start.21 = (bf16[768]{0:T(1024)(128)(2,1)S(1)}, bf16[768]{0:T(1024)(128)(2,1)}, u32[]{:S(2)}) copy-start(bf16[768]{0:T(1024)(128)(2,1)} %param.61) | copy-start | bytes 4612
  10.6 5.3 %copy-start.22 = (bf16[768]{0:T(1024)(128)(2,1)S(1)}, bf16[768]{0:T(1024)(128)(2,1)}, u32[]{:S(2)}) copy-start(bf16[768]{0:T(1024)(128)(2,1)} %param.64) | copy-start | bytes 4612
  10.6 6.7 %copy-start.10 = (bf16[262,768]{1,0:T(8,128)(2,1)S(1)}, bf16[262,768]{1,0:T(8,128)(2,1)}, u32[]{:S(2)}) copy-start(bf16[262,768]{1,0:T(8,128)(2,1)} %param.36) | copy-start | bytes 1207300
  10.9 12.0 %copy-start.4 = (bf16[256,1280]{1,0:T(8,128)(2,1)}, bf16[256,1280]{1,0:T(8,128)(2,1)S(1)}, u32[]{:S(2)}) copy-start(bf16[256,1280]{1,0:T(8,128)(2,1)S(1)} %fusion.9.refs_15_.refs_9_) | copy-start | bytes 1966084
  11.3 11.6 %copy-start.12 = (bf16[256,256]{1,0:T(8,128)(2,1)}, bf16[256,256]{1,0:T(8,128)(2,1)S(1)}, u32[]{:S(2)}) copy-start(bf16[256,256]{1,0:T(8,128)(2,1)S(1)} %convolution_convert_fusion.1.refs_12_) | copy-start | bytes 393220
  11.6 19.1 %copy-start.8 = (bf16[256,768]{1,0:T(8,128)(2,1)}, bf16[256,768]{1,0:T(8,128)(2,1)S(1)}, u32[]{:S(2)}) copy-start(bf16[256,768]{1,0:T(8,128)(2,1)S(1)} %convolution_convert_fusion.refs_3_) | copy-start | bytes 1179652
  23.0 2.7 copy-start
  25.7 17.3 %collective-permute-start.1 = (bf16[262,1024]{1,0:T(8,128)(2,1)}, bf16[262,1024]{1,0:T(8,128)(2,1)}, u32[]{:S(2)}, u32[]{:S(2)}) collective-permute-start(bf16[262,1024]{1,0:T(8,128)(2,1)} %shard_map.544), channel_id=1, source_target_pairs={{0,1},{1,0},{2,3},{3,2},{4,5},{5,4},{6,7},{7,6},{8,9},{9,8},{10,11... | collective-permute-start | bytes 1609736 | tf_op jit(solution)/shard_map/ppermute | solution.py:875
  30.8 2.4 copy-start.3
  38.5 3.5 %copy-start.1 = (f32[256,2048]{1,0:T(8,128)S(1)}, f32[256,2048]{1,0:T(8,128)}, u32[]{:S(2)}) copy-start(f32[256,2048]{1,0:T(8,128)} %get-tuple-element.219) | copy-start | bytes 6291460
  38.5 4.5 %copy-start.7 = (bf16[2,1024,262]{1,2,0:T(8,128)(2,1)S(1)}, bf16[2,1024,262]{1,2,0:T(8,128)(2,1)}, u32[]{:S(2)}) copy-start(bf16[2,1024,262]{1,2,0:T(8,128)(2,1)} %copy-done.6) | copy-start | bytes 3219460
  104.1 3.5 %copy-start.2 = (f32[256,2048]{1,0:T(8,128)S(1)}, f32[256,2048]{1,0:T(8,128)}, u32[]{:S(2)}) copy-start(f32[256,2048]{1,0:T(8,128)} %get-tuple-element.219) | copy-start | bytes 6291460
  105.5 217.4 %collective-permute-start.2 = (bf16[262,1024]{1,0:T(8,128)(2,1)S(1)}, bf16[262,1024]{1,0:T(8,128)(2,1)S(1)}, u32[]{:S(2)}, u32[]{:S(2)}) collective-permute-start(bf16[262,1024]{1,0:T(8,128)(2,1)S(1)} %get-tuple-element.209), channel_id=1, source_target_pairs={{0,1},{1,0},{2,3},{3,2},{4,5},{5,4},{6,7},{7,6},{8,9},{9,8},{10,11... | collective-permute-start | bytes 1609736 | tf_op jit(solution)/shard_map/ppermute | solution.py:875

commit v2 on v1

--- a/solution.py
+++ b/solution.py
@@ -530,6 +530,58 @@
     return rstd * (dhat - first - hat * second)
 
 
+def lookup_kernel(scale, codes, table, position, gain, qk, nb, rstd_out, soft, p, pn, scores):
+    i = pl.program_id(0)
+    block = codes.shape[1]
+    rows = pl.ds(pl.multiple_of(i * block, block), block)
+    entry = lax.broadcasted_iota(jnp.int32, (table.shape[0], block), 0)
+    onehot = (entry == codes[...]).astype(BF16)
+    hat, rstd = center(nn(onehot.T, table[...]) + position[...].astype(F32))
+    normed = (hat * gain[...].astype(F32)).astype(BF16)
+    nb[rows, :] = normed
+    rstd_out[...] = rstd
+    scores[:, rows] = nt(qk[...], normed) * scale
+
+    @pl.when(i == pl.num_programs(0) - 1)
+    def _():
+        soft[...] = softmax(scores[...])
+        p[...] = soft[...].astype(BF16)
+        pn[...] = nn(p[...], nb[...]).astype(BF16)
+
+
+def bytes_forward(codes, table, position, gain, qk, scale):
+    rows, width = position.shape
+    latents, block = qk.shape[0], 256
+
+    def whole(x):
+        return pl.BlockSpec(x.shape, lambda i: (0, 0))
+
+    shapes = [
+        jax.ShapeDtypeStruct((rows, width), BF16),
+        jax.ShapeDtypeStruct((rows, 1), F32),
+        jax.ShapeDtypeStruct((latents, rows), F32),
+        jax.ShapeDtypeStruct((latents, rows), BF16),
+        jax.ShapeDtypeStruct((latents, width), BF16),
+    ]
+    specs = [whole(x) for x in shapes]
+    specs[1] = pl.BlockSpec((block, 1), lambda i: (i, 0))
+    return pl.pallas_call(
+        lambda *refs: lookup_kernel(scale, *refs),
+        grid=(rows // block,),
+        out_shape=shapes,
+        in_specs=[
+            pl.BlockSpec((1, block), lambda i: (0, i)),
+            whole(table),
+            pl.BlockSpec((block, width), lambda i: (i, 0)),
+            pl.BlockSpec((1, width), lambda i: (0, 0)),
+            whole(qk),
+        ],
+        out_specs=specs,
+        scratch_shapes=[pltpu.VMEM((latents, rows), F32)],
+        compiler_params=pltpu.CompilerParams(vmem_limit_bytes=48 * 1024 * 1024),
+    )(codes[None, :], table, position, gain[None, :], qk)
+
+
 def bytes_kernel(
     at, scale, p, soft, vd, qk, nb, rstd, gain, codes, emb, sums, wide,
     pn, q, dae, daft, nl, rstd_l, gain_l, w_key, w_query,
@@ -900,18 +952,14 @@
     table = jnp.concatenate(
         [embedding, mask_vector[None, :], jnp.zeros((padded - vocab - 1, embedding.shape[1]), BF16)], axis=0
     )
-    onehot = (codes[:, None] == lax.iota(jnp.int32, padded)[None, :]).astype(BF16)
-    bytes_in = nn(onehot, table) + position.astype(F32)
-    nb, hat_b, rstd_b = norm_forward(bytes_in, gain_bytes)
 
     latent32 = latent_init.astype(F32)
     nl, hat_l, rstd_l = norm_forward(latent32, gain_latent)
     q_e = nn(nl, query_enc).astype(BF16)
     scale_e = q_e.shape[1] ** (-0.5)
     qk_e = nt(q_e, key_enc).astype(BF16)
-    soft_e = softmax(nt(qk_e, nb) * scale_e)
-    p_e = soft_e.astype(BF16)
-    pn_e = nn(p_e, nb).astype(BF16)
+    nb, rstd_b, soft_e, p_e, pn_e = bytes_forward(codes, table, position, gain_bytes, qk_e, scale_e)
+
     gains = (gain_enc_mlp, gain_self, gain_self_mlp, gain_dec_kv)
     (
         a_e, n1, h1, n2, a_s, n3, h2, n4,

time: 331 us -> 319 us (0.964)
  other arithmetic: 24 us -> 11.1 us
  Pallas kernels: 277 us -> 285 us
  matrix products: 7.1 us -> 0.64 us
    pallas_call x0 -> x1, Pallas kernels: none -> 13 us  [bytes_forward(): pl.pallas_call(lambda *refs: lookup_kernel(scale, *refs), grid=(rows // b...]
    unnamed x1 -> x0, Pallas kernels: 5.32 us -> none
    convert_element_type x4 -> x2, other arithmetic: 6.06 us -> 0.97 us  [norm_forward(): return ((hat * gain.astype(F32)).astype(BF16), hat, rstd)]
    convert_element_type x2 -> x0, other arithmetic: 4.22 us -> none  [the longest x1 2.15 us: local(): p_e = soft_e.astype(BF16)]
    dot_general x2 -> x1, matrix products: 4.46 us -> 0.34 us  [nn(): lax.dot_general(a, b, (((1,), (0,)), ((), ())), preferred_element_type=F32)]
  transfers between devices with their start and end apart: 3 -> 3, of which waited for: 0 -> 0; matrix products, arithmetic and copies ran while one was open for 8% -> 4% of each run, Pallas kernels for 67% -> 72%
where the time goes in v2:
time: 319 us; the launch traced here: 315 us
  Pallas kernels  285 us (89%)
  local copies, waits for them, and re-layouts  11.4 us (4%)
  other arithmetic  11.1 us (3%)
  starting transfers between devices  5.12 us (2%)
    pallas_call x1, Pallas kernels, reduce_all(): pl.pallas_call(lambda *refs: reduce_kernel(plan, *refs), out_shape=[jax.S...  189 us
    pallas_call x1, Pallas kernels, streamed(): pl.pallas_call(kernel, out_shape=shapes, in_specs=[pl.BlockSpec(memory_sp...  58.8 us
    pallas_call x1, Pallas kernels, bytes_backward(): pl.pallas_call(lambda *refs: bytes_kernel(at, scale, *refs), grid=(rows /...  19.7 us
    pallas_call x1, Pallas kernels, bytes_forward(): pl.pallas_call(lambda *refs: lookup_kernel(scale, *refs), grid=(rows // b...  13 us
  transfers between devices with their start and end apart: 3, of which 0 were waited for; matrix products, arithmetic and copies ran while one was open for 4% of the time, Pallas kernels for 72%

profile of v2, /device:TPU:0, one launch (start us, length us, event | category | flops | bytes accessed | tf_op | source)
XLA Modules:
  0.0 314.6 jit_solution(13816524894360732413)
XLA Ops:
  0.7 0.0 copy-start.15
  0.7 0.8 broadcast_select_fusion.4
  1.5 3.0 collective-permute-start
  4.5 0.7 broadcast_in_dim.76
  5.2 0.7 convert_element_type.20
  5.9 1.3 convert_reduce_fusion
  7.2 1.4 fusion.4
  8.6 0.0 copy-done.15
  8.6 0.3 copy.70
  8.9 0.0 copy-start.9
  8.9 0.0 copy-start.25
  8.9 0.0 copy-start.8
  8.9 1.0 copy-done.9
  9.9 0.9 select_bitcast_fusion.1.refs_0_
  10.8 0.1 pad.16.clone
  10.8 0.3 fusion.6.refs_15_.refs_9_
  11.1 0.1 copy-done.11
  11.2 0.0 copy-start.18
  11.2 0.0 copy-start.19
  11.2 0.0 copy-start.20
  11.3 0.0 copy-start.22
  11.3 0.0 copy-start.23
  11.3 0.3 convolution_convert_fusion.1.refs_12_
  11.6 0.3 copy-done.12
  11.9 0.1 maximum_maximum_fusion.refs_1_
  12.1 0.8 pad.8.refs_22_
  12.9 0.0 copy-start.6
  12.9 0.6 broadcast_in_dim.79.refs_2_
  13.5 0.0 copy-done.18
  13.5 0.6 broadcast_in_dim.80.refs_3_
  14.1 0.6 broadcast_in_dim.81.refs_4_
  14.7 0.6 broadcast_in_dim.82.refs_5_
  15.3 0.6 broadcast_in_dim.83.refs_6_
  15.9 0.6 broadcast_in_dim.84.refs_7_
  16.5 0.0 collective-permute-done
  16.5 0.6 pad_add_fusion.refs_1_
  17.1 0.0 collective-permute-start.1
  17.1 0.1 fusion.9
  17.2 0.3 convolution_convert_fusion.refs_4_.refs_3_
  17.5 0.0 copy-start.5
  17.6 13.0 %shard_map.544 = (bf16[2048,768]{1,0:T(8,128)(2,1)}, f32[2048,1]{1,0:T(8,128)S(1)}, f32[256,2048]{1,0:T(8,128)S(1)}, bf16[256,2048]{1,0:T(8,128)(2,1)S(1)}, bf16[256,768]{1,0:T(8,128)(2,1)S(1)}) custom-call(s32[1,2048]{1,0:T(1,128)S(1)} %reshape_select_fusion.refs_0_.refs_7_, bf16[384,768]{1,0:T(8,128)(2,1)S(1)} %maximum_maximum_fusion.refs_1_, ...), custom_call_target="tpu_custom_call" | custom-call | tf_op jit(solution)/shard_map/pallas_call | solution.py:568
  30.5 0.0 copy-done.6
  30.5 0.0 copy-done
  30.6 0.0 copy-done.5
  30.6 0.0 copy-start.3
  30.6 1.0 copy-done.3
  31.5 1.0 copy-done.4
  32.5 0.0 collective-permute-done.1
  32.5 0.1 bitcast_select_fusion.1
  32.6 1.2 copy-done.1
  33.8 0.1 copy-done.2
  33.9 1.1 fusion.7.refs_24_
  35.1 58.8 %shard_map.546 = (bf16[256,1280]{1,0:T(8,128)(2,1)}, bf16[256,1280]{1,0:T(8,128)(2,1)}, bf16[256,1280]{1,0:T(8,128)(2,1)}, bf16[256,1280]{1,0:T(8,128)(2,1)}, bf...) custom-call(bf16[256,1280]{1,0:T(8,128)(2,1)} %refs_0_.1, ...), custom_call_target="tpu_custom_call" | custom-call | tf_op jit(solution)/shard_map/pallas_call | solution.py:761
  93.9 0.0 copy-start.16
  93.9 1.3 select_bitcast_fusion
  95.2 2.1 collective-permute-start.2
  97.3 0.0 copy-done.16
  97.3 0.6 broadcast_in_dim.89.refs_17_
  97.9 0.8 copy.68.refs_16_
  98.7 19.7 %shard_map.547 = (bf16[2048,768]{1,0:T(8,128)(2,1)}, bf16[768,384]{1,0:T(8,128)(2,1)}, bf16[1280,128]{1,0:T(8,128)(2,1)}, bf16[256,256]{1,0:T(8,128)(2,1)}, bf16...) custom-call(bf16[256,2048]{1,0:T(8,128)(2,1)} %copy-done.4, f32[256,2048]{1,0:T(8,128)} %copy-done.1, ...), custom_call_target="tpu_custom_call" | custom-call | tf_op jit(solution)/shard_map/pallas_call | solution.py:654
  118.3 189.4 %shard_map.548 = (f32[40,1280]{1,0:T(8,128)}, f32[40,1280]{1,0:T(8,128)}, f32[40,1280]{1,0:T(8,128)}, f32[40,1280]{1,0:T(8,128)}, f32[40,256]{1,0:T(8,128)}, /*i...) custom-call(bf16[256,1280]{1,0:T(8,128)(2,1)} %get-tuple-element.123, ...), custom_call_target="tpu_custom_call" | custom-call | tf_op jit(solution)/shard_map/pallas_call | solution.py:463
  307.7 4.3 %shard_map.549 = (f32[64,768]{1,0:T(8,128)}, f32[24,256]{1,0:T(8,128)}, f32[24,1280]{1,0:T(8,128)}, f32[8,1280]{1,0:T(8,128)}, f32[40,256]{1,0:T(8,128)}, /*inde...) custom-call(f32[64,768]{1,0:T(8,128)} %get-tuple-element.162.refs_0_, ...), custom_call_target="tpu_custom_call" | custom-call | tf_op jit(solution)/shard_map/pallas_call | solution.py:511
  312.0 0.0 collective-permute-done.2
  312.0 2.4 broadcast_select_fusion
  (36 shorter events, 0.1 us)
Async XLA Ops:
  0.7 7.9 %copy-start.15 = (bf16[2,1024,262]{1,0,2:T(2,128)(2,1)S(1)}, bf16[2,1024,262]{1,0,2:T(2,128)(2,1)}, u32[]{:S(2)}) copy-start(bf16[2,1024,262]{1,0,2:T(2,128)(2,1)} %param.65) | copy-start | bytes 3219460
  1.5 15.0 %collective-permute-start = (s32[1024]{0:T(1024)S(1)}, s32[1024]{0:T(1024)S(1)}, u32[]{:S(2)}, u32[]{:S(2)}) collective-permute-start(s32[1024]{0:T(1024)S(1)} %bitcast.52), channel_id=1, source_target_pairs={{0,1},{1,0},{2,3},{3,2},{4,5},{5,4},{6,7},{7,6},{8,9},{9,8},{10,11... | collective-permute-start | bytes 12296 | tf_op jit(solution)/shard_map/ppermute | solution.py:927
  8.9 1.0 copy-start.9
  8.9 1.9 copy-start.25
  8.9 1.9 copy-start.8
  9.9 1.3 copy-start.11
  10.8 1.1 copy-start.12
  11.2 1.6 copy-start.7
  11.2 0.8 copy-start.24
  11.2 1.6 copy-start.21
  11.2 1.6 copy-start.17
  11.2 2.3 copy-start.18
  11.2 2.9 copy-start.19
  11.2 3.4 %copy-start.20 = (bf16[1280]{0:T(1024)(128)(2,1)S(1)}, bf16[1280]{0:T(1024)(128)(2,1)}, u32[]{:S(2)}) copy-start(bf16[1280]{0:T(1024)(128)(2,1)} %param.57) | copy-start | bytes 7684
  11.3 4.0 %copy-start.22 = (bf16[768]{0:T(1024)(128)(2,1)S(1)}, bf16[768]{0:T(1024)(128)(2,1)}, u32[]{:S(2)}) copy-start(bf16[768]{0:T(1024)(128)(2,1)} %param.61) | copy-start | bytes 4612
  11.3 4.6 %copy-start.23 = (bf16[768]{0:T(1024)(128)(2,1)S(1)}, bf16[768]{0:T(1024)(128)(2,1)}, u32[]{:S(2)}) copy-start(bf16[768]{0:T(1024)(128)(2,1)} %param.64) | copy-start | bytes 4612
  11.9 5.3 %copy-start.14 = (bf16[256,256]{1,0:T(8,128)(2,1)}, bf16[256,256]{1,0:T(8,128)(2,1)S(1)}, u32[]{:S(2)}) copy-start(bf16[256,256]{1,0:T(8,128)(2,1)S(1)} %convolution_convert_fusion.1.refs_12_) | copy-start | bytes 393220
  11.9 5.3 %copy-start.13 = (bf16[768,256]{1,0:T(8,128)(2,1)S(1)}, bf16[768,256]{1,0:T(8,128)(2,1)}, u32[]{:S(2)}) copy-start(bf16[768,256]{1,0:T(8,128)(2,1)} %refs_18_.3) | copy-start | bytes 1179652
  12.9 17.7 %copy-start.6 = (bf16[1,768]{1,0:T(2,128)(2,1)}, bf16[1,768]{1,0:T(2,128)(2,1)S(1)}, u32[]{:S(2)}) copy-start(bf16[1,768]{1,0:T(2,128)(2,1)S(1)} %broadcast_in_dim.78.refs_3_.refs_6_) | copy-start | bytes 4612
  17.1 15.4 %collective-permute-start.1 = (bf16[262,1024]{1,0:T(8,128)(2,1)}, bf16[262,1024]{1,0:T(8,128)(2,1)S(1)}, u32[]{:S(2)}, u32[]{:S(2)}) collective-permute-start(bf16[262,1024]{1,0:T(8,128)(2,1)} %shard_map.545), channel_id=1, source_target_pairs={{0,1},{1,0},{2,3},{3,2},{4,5},{5,4},{6,7},{7,6},{8,9},{9,8},{10,11... | collective-permute-start | bytes 1609736 | tf_op jit(solution)/shard_map/ppermute | solution.py:927
  17.5 13.0 %copy-start = (bf16[256,768]{1,0:T(8,128)(2,1)}, bf16[256,768]{1,0:T(8,128)(2,1)S(1)}, u32[]{:S(2)}) copy-start(bf16[256,768]{1,0:T(8,128)(2,1)S(1)} %convolution_convert_fusion.refs_4_.refs_3_) | copy-start | bytes 1179652
  17.5 13.0 %copy-start.5 = (s32[1,2048]{1,0:T(1,128)}, s32[1,2048]{1,0:T(1,128)S(1)}, u32[]{:S(2)}) copy-start(s32[1,2048]{1,0:T(1,128)S(1)} %reshape_select_fusion.refs_0_.refs_7_) | copy-start | bytes 24580
  17.6 15.0 %copy-start.10 = (bf16[2,1024,262]{1,2,0:T(8,128)(2,1)S(1)}, bf16[2,1024,262]{1,2,0:T(8,128)(2,1)}, u32[]{:S(2)}) copy-start(bf16[2,1024,262]{1,2,0:T(8,128)(2,1)} %copy-done.9) | copy-start | bytes 3219460
  30.6 1.0 copy-start.3
  31.5 1.0 copy-start.4
  32.5 1.3 copy-start.1
  32.5 1.4 copy-start.2
  93.9 3.4 %copy-start.16 = (bf16[1280]{0:T(1024)(128)(2,1)S(1)}, bf16[1280]{0:T(1024)(128)(2,1)}, u32[]{:S(2)}) copy-start(bf16[1280]{0:T(1024)(128)(2,1)} %param.43) | copy-start | bytes 7684
  95.2 216.8 %collective-permute-start.2 = (bf16[262,1024]{1,0:T(8,128)(2,1)S(1)}, bf16[262,1024]{1,0:T(8,128)(2,1)S(1)}, u32[]{:S(2)}, u32[]{:S(2)}) collective-permute-start(bf16[262,1024]{1,0:T(8,128)(2,1)S(1)} %get-tuple-element.215), channel_id=1, source_target_pairs={{0,1},{1,0},{2,3},{3,2},{4,5},{5,4},{6,7},{7,6},{8,9},{9,8},{10,11... | collective-permute-start | bytes 1609736 | tf_op jit(solution)/shard_map/ppermute | solution.py:927

commit v3 on v2

--- a/solution.py
+++ b/solution.py
@@ -54,7 +54,7 @@
 
 def softmax(s):
     e = jnp.exp(s - jnp.max(s, axis=-1, keepdims=True))
-    return e / jnp.sum(e, axis=-1, keepdims=True)
+    return e * (1.0 / jnp.sum(e, axis=-1, keepdims=True))
 
 
 def softmax_backward(dp, soft, scale):
@@ -539,7 +539,7 @@
     hat, rstd = center(nn(onehot.T, table[...]) + position[...].astype(F32))
     normed = (hat * gain[...].astype(F32)).astype(BF16)
     nb[rows, :] = normed
-    rstd_out[...] = rstd
+    rstd_out[...] = jnp.broadcast_to(rstd, (block, 128)).T[:1]
     scores[:, rows] = nt(qk[...], normed) * scale
 
     @pl.when(i == pl.num_programs(0) - 1)
@@ -558,13 +558,13 @@
 
     shapes = [
         jax.ShapeDtypeStruct((rows, width), BF16),
-        jax.ShapeDtypeStruct((rows, 1), F32),
+        jax.ShapeDtypeStruct((1, rows), F32),
         jax.ShapeDtypeStruct((latents, rows), F32),
         jax.ShapeDtypeStruct((latents, rows), BF16),
         jax.ShapeDtypeStruct((latents, width), BF16),
     ]
     specs = [whole(x) for x in shapes]
-    specs[1] = pl.BlockSpec((block, 1), lambda i: (i, 0))
+    specs[1] = pl.BlockSpec((1, block), lambda i: (0, i))
     return pl.pallas_call(
         lambda *refs: lookup_kernel(scale, *refs),
         grid=(rows // block,),
@@ -582,86 +582,6 @@
     )(codes[None, :], table, position, gain[None, :], qk)
 
 
-def bytes_kernel(
-    at, scale, p, soft, vd, qk, nb, rstd, gain, codes, emb, sums, wide,
-    pn, q, dae, daft, nl, rstd_l, gain_l, w_key, w_query,
-    dbytes, table, turned, dq, g_key, g_value, g_latent,
-    total, ds,
-):
-    i = pl.program_id(0)
-    block = codes.shape[1]
-
-    @pl.when(i == 0)
-    def _():
-        total[...] = jnp.zeros_like(total)
-        total[: emb.shape[0]] = emb[...]
-        total[at + 1 : at + 2] = sums[1:2]
-        total[at + 2 : at + 3] = sums[0:1]
-        ds[...] = softmax_backward(nt(vd[...], nb[...]), soft[...], scale)
-        dn = nn(ds[...], nb[...]).astype(BF16)
-        g_key[...] = nn(dn.T, q[...]).astype(BF16)
-        g_value[...] = nn(pn[...].T, dae[...]).astype(BF16)
-        dq[...] = nn(dn, w_key[...]).astype(BF16)
-        dnl = nt(dq[...], w_query[...])
-        g = gain_l[...].astype(F32)
-        hat = nl[...].astype(F32) / g
-        g_latent[...] = (daft[...] + center_backward(dnl * g, hat, rstd_l[...])).astype(BF16)
-        first = jnp.sum(dnl * hat, axis=0, keepdims=True)
-        own = lax.broadcasted_iota(jnp.int32, wide.shape, 0) == 0
-        turned[...] = jnp.zeros_like(turned)
-        turned[:, : wide.shape[0]] = jnp.where(own, first, wide[...]).T.astype(BF16)
-
-    rows = pl.ds(pl.multiple_of(i * block, block), block)
-    g = gain[...].astype(F32)
-    normed = nb[rows, :]
-    dnb = nn(p[...].T, vd[...]) + nn(ds[:, rows].T, qk[...])
-    hat = normed.astype(F32) / g
-    dx = center_backward(dnb * g, hat, rstd[...]).astype(BF16)
-    dbytes[...] = dx
-    entry = lax.broadcasted_iota(jnp.int32, (total.shape[0], block), 0)
-    onehot = (entry == codes[...]).astype(BF16)
-    total[...] += nn(onehot, dx)
-    total[at : at + 1] += jnp.sum(dnb * hat, axis=0, keepdims=True)
-
-    @pl.when(i == pl.num_programs(0) - 1)
-    def _():
-        table[...] = total[...].T.astype(BF16)
-
-
-def bytes_backward(at, scale, p, soft, vd, qk, nb, rstd, gain, codes, emb, sums, wide, rest):
-    rows, width = nb.shape
-    latents, block, entries = p.shape[0], 256, -(-emb.shape[0] // 128) * 128
-    features = wide.shape[1]
-    qk_width = rest[1].shape[1]
-
-    def whole(x):
-        return pl.BlockSpec(x.shape, lambda i: (0, 0))
-
-    shapes = [
-        jax.ShapeDtypeStruct((rows, width), BF16),
-        jax.ShapeDtypeStruct((width, entries), BF16),
-        jax.ShapeDtypeStruct((features, 128), BF16),
-        jax.ShapeDtypeStruct((latents, qk_width), BF16),
-        jax.ShapeDtypeStruct((width, qk_width), BF16),
-        jax.ShapeDtypeStruct((width, features), BF16),
-        jax.ShapeDtypeStruct((latents, features), BF16),
-    ]
-    arrays = (p, soft, vd, qk, nb, rstd, gain[None, :], codes[None, :], emb, sums, wide) + rest
-    specs = [whole(x) for x in arrays]
-    specs[0] = pl.BlockSpec((latents, block), lambda i: (0, i))
-    specs[5] = pl.BlockSpec((block, 1), lambda i: (i, 0))
-    specs[7] = pl.BlockSpec((1, block), lambda i: (0, i))
-    return pl.pallas_call(
-        lambda *refs: bytes_kernel(at, scale, *refs),
-        grid=(rows // block,),
-        out_shape=shapes,
-        in_specs=specs,
-        out_specs=[pl.BlockSpec((block, width), lambda i: (i, 0))] + [whole(x) for x in shapes[1:]],
-        scratch_shapes=[pltpu.VMEM((entries, width), F32), pltpu.VMEM((latents, rows), BF16)],
-        compiler_params=pltpu.CompilerParams(vmem_limit_bytes=60 * 1024 * 1024),
-    )(*arrays)
-
-
 def head_columns(head, width):
     each = width // HEADS
     low, high = head * each // 128 * 128, -(-(head + 1) * each // 128) * 128
@@ -769,6 +689,90 @@
         + extra,
         compiler_params=pltpu.CompilerParams(vmem_limit_bytes=63 * 1024 * 1024),
     )(*small, *large)
+
+
+def bytes_backward(at, scale, arrays):
+    vd, nb, soft, q, w_key, w_query, latent = arrays[:7]
+    rows, width = nb.shape
+    latents, features = latent.shape
+    entries, block = -(-arrays[12].shape[0] // 128) * 128, 256
+    steps = rows // block
+
+    def body(small, w, results, extra):
+        ds, turned, total, table, dq, g_key, g_value, g_latent, row_sem = extra
+        vd, nb = w[0], w[1]
+        ds[...] = softmax_backward(nt(vd, nb), w[2], scale)
+        dn = nn(ds[...], nb).astype(BF16)
+        g_key[...] = nn(dn.T, w[3]).astype(BF16)
+        results.send(g_key)
+        dq[...] = nn(dn, w[4]).astype(BF16)
+        results.send(dq)
+        dnl = nt(dq[...], w[5])
+        hat, rstd = center(w[6].astype(F32))
+        g = w[10].astype(F32)
+        g_latent[...] = (w[7] + center_backward(dnl * g, hat, rstd)).astype(BF16)
+        results.send(g_latent)
+        g_value[...] = nn(w[8].T, w[9]).astype(BF16)
+        results.send(g_value)
+        first = jnp.sum(dnl * hat, axis=0, keepdims=True)
+        own = lax.broadcasted_iota(jnp.int32, (8, features), 0) == 0
+        turned[...] = jnp.zeros_like(turned)
+        turned[:, :8] = jnp.where(own, first, w[11]).T.astype(BF16)
+        results.send(turned)
+        emb, sums = w[12], w[13]
+        total[...] = jnp.zeros_like(total)
+        total[: emb.shape[0]] = emb
+        total[at + 1 : at + 2] = sums[1:2]
+        total[at + 2 : at + 3] = sums[0:1]
+        qk, g = w[15], w[18].astype(F32)
+        inverse = 1.0 / g
+        w[14], w[16], w[17]
+        p_ref, scale_ref, codes_ref, nb_ref = w.targets[14], w.targets[16], w.targets[17], w.targets[1]
+        target = results.targets[6]
+
+        def out_copy(i):
+            here = pl.ds(pl.multiple_of(i * block, block), block)
+            return pltpu.make_async_copy(nb_ref.at[here], target.at[here], row_sem.at[i])
+
+        def step(i, carry):
+            here = pl.ds(pl.multiple_of(i * block, block), block)
+            rstd = jnp.broadcast_to(scale_ref[:, here], (128, block)).T[:, :1]
+            normed = nb_ref[here, :]
+            dnb = nn(p_ref[:, here].T, vd) + nn(ds[:, here].T, qk)
+            hat = normed.astype(F32) * inverse
+            dx = center_backward(dnb * g, hat, rstd).astype(BF16)
+            nb_ref[here, :] = dx
+            out_copy(i).start()
+            entry = lax.broadcasted_iota(jnp.int32, (entries, block), 0)
+            onehot = (entry == codes_ref[:, here]).astype(BF16)
+            total[...] += nn(onehot, dx)
+            total[at : at + 1] += jnp.sum(dnb * hat, axis=0, keepdims=True)
+            return carry
+
+        lax.fori_loop(0, steps, step, 0)
+        table[...] = total[...].T.astype(BF16)
+        results.send(table)
+
+        def wait(i, carry):
+            out_copy(i).wait()
+            return carry
+
+        lax.fori_loop(0, steps, wait, 0)
+
+    qk_width = q.shape[1]
+
+    def low(*shape):
+        return jax.ShapeDtypeStruct(shape, BF16)
+
+    shapes = [
+        low(width, qk_width), low(latents, qk_width), low(latents, features), low(width, features),
+        low(features, 128), low(width, entries), low(rows, width),
+    ]
+    vmem = pltpu.VMEM
+    extra = [vmem((latents, rows), BF16), vmem((features, 128), BF16), vmem((entries, width), F32)]
+    extra += [vmem((width, entries), BF16), vmem((latents, qk_width), BF16), vmem((width, qk_width), BF16)]
+    extra += [vmem((width, features), BF16), vmem((latents, features), BF16), pltpu.SemaphoreType.DMA((steps,))]
+    return streamed(body, [], arrays, shapes, extra, set(range(len(shapes))))
 
 
 def middle_pass(latent, pn, gains, byte_gains, weights, scale):
@@ -845,7 +849,10 @@
 
         lax.fori_loop(0, queries.shape[0] // block, decode, 0)
         results.send(query_ref)
-        results.send(cot_ref)
+        half = queries.shape[0] // 2
+        mine = lax.axis_index("blk")
+        for part in (mine, 1 - mine):
+            results.send(cot_ref.at[:, pl.ds(pl.multiple_of(part * half, half), half)])
         results.send(g_emb)
         results.send(g_byte)
         pd, dn = g_pd[...].astype(BF16), g_dn[...].astype(BF16)
@@ -860,7 +867,7 @@
 
         def back(dy, normed, rstd, gain, row):
             g = gain[...].astype(F32)
-            hat = normed[...].astype(F32) / g
+            hat = normed[...].astype(F32) * (1.0 / g)
             sums[row : row + 1] = jnp.sum(dy * hat, axis=0, keepdims=True)
             return center_backward(dy * g, hat, rstd)
 
@@ -893,11 +900,12 @@
         return jax.ShapeDtypeStruct(shape, F32)
 
     shapes = [low(*wide)] * 8
-    shapes += [low(*queries.shape), low(*cot.shape), full(entries, depth), full(8, depth)]
+    shapes += [low(*queries.shape)] + [low(entries, queries.shape[0] // 2)] * 2
+    shapes += [full(entries, depth), full(8, depth)]
     shapes += [low(rows, qk), low(rows, depth), low(depth, qk), low(depth, depth)]
     shapes += [low(*wide)] * 3 + [low(rows, qk)] * 2 + [low(*wide)] * 4
     shapes += [full(*wide), low(*wide), low(rows, depth), full(8, width)]
-    unstaged = {8, 9, 10, 11, 16, 17, 18, 21, 22, 23, 24, 25, 26, 28}
+    unstaged = {8, 9, 10, 11, 12, 17, 18, 19, 22, 23, 24, 25, 26, 27, 29}
     vmem = pltpu.VMEM
     extra = [vmem(wide, F32), vmem((rows, qk), F32), vmem((rows, qk), F32), vmem((8, width), F32)]
     extra += [vmem(wide, F32)] * 2 + [vmem((rows, qk), BF16)] * 2 + [vmem(wide, BF16)]
@@ -954,7 +962,7 @@
     )
 
     latent32 = latent_init.astype(F32)
-    nl, hat_l, rstd_l = norm_forward(latent32, gain_latent)
+    nl = norm_forward(latent32, gain_latent)[0]
     q_e = nn(nl, query_enc).astype(BF16)
     scale_e = q_e.shape[1] ** (-0.5)
     qk_e = nt(q_e, key_enc).astype(BF16)
@@ -963,7 +971,7 @@
     gains = (gain_enc_mlp, gain_self, gain_self_mlp, gain_dec_kv)
     (
         a_e, n1, h1, n2, a_s, n3, h2, n4,
-        g_dec_query, logits, g_emb_out, gain_sums, dk_d, dv_d, g_query_dec, g_out_dec,
+        g_dec_query, logits_own, logits_other, g_emb_out, gain_sums, dk_d, dv_d, g_query_dec, g_out_dec,
         dlat16, du2, das16, dq_s, dk_s, dv_s, denc16, du1, daft16, dafter, dae16, vd_e, wide,
     ) = middle_pass(
         latent_init, pn_e, gains, (gain_dec_q, gain_final),
@@ -973,15 +981,16 @@
         ],
         query_dec.shape[1] ** (-0.5),
     )
-    logits = logits[:vocab]
-    logits_got = swap(jnp.where(me == 0, logits[:, half:], logits[:, :half]))
-    logits_own = jnp.where(me == 0, logits[:, :half], logits[:, half:])
+    logits_own, logits_got = logits_own[:vocab], swap(logits_other)[:vocab]
     side = lax.broadcasted_iota(jnp.int32, (1, 2, 1), 1)
     logits_out = jnp.where(side == me, logits_own[:, None, :], logits_got[:, None, :]).transpose(1, 2, 0)
 
-    dbytes, g_table, vectors, dq_e, g_key_enc, g_value_enc, g_latent = bytes_backward(
-        vocab + 1, scale_e, p_e, soft_e, vd_e, qk_e, nb, rstd_b, gain_bytes, codes, g_emb_out, gain_sums, wide,
-        (pn_e, q_e, dae16, dafter, nl, rstd_l, gain_latent[None, :], key_enc, query_enc),
+    g_key_enc, dq_e, g_latent, g_value_enc, vectors, g_table, dbytes = bytes_backward(
+        vocab + 1, scale_e,
+        [
+            vd_e, nb, soft_e, q_e, key_enc, query_enc, latent_init, dafter, pn_e, dae16, gain_latent[None, :], wide,
+            g_emb_out, gain_sums, p_e, qk_e, rstd_b, codes[None, :], gain_bytes[None, :],
+        ],
     )
 
     def low(g):

time: 319 us -> 314 us (0.984)
    pallas_call x1 -> x0, Pallas kernels: 19.7 us -> none  [bytes_backward(): pl.pallas_call(lambda *refs: bytes_kernel(at, scale, *refs), grid=(rows /...]
    pallas_call x1 -> x2, Pallas kernels: 58.8 us -> 76.5 us  [streamed(): pl.pallas_call(kernel, out_shape=shapes, in_specs=[pl.BlockSpec(memory_sp...]
where the time goes in v3:
time: 314 us; the launch traced here: 310 us
  Pallas kernels  283 us (90%)
  other arithmetic  9.8 us (3%)
  local copies, waits for them, and re-layouts  9.78 us (3%)
  starting transfers between devices  5.12 us (2%)
    pallas_call x1, Pallas kernels, reduce_all(): pl.pallas_call(lambda *refs: reduce_kernel(plan, *refs), out_shape=[jax.S...  189 us
    pallas_call x2, Pallas kernels, streamed(): pl.pallas_call(kernel, out_shape=shapes, in_specs=[pl.BlockSpec(memory_sp...  76.5 us
    pallas_call x1, Pallas kernels, bytes_forward(): pl.pallas_call(lambda *refs: lookup_kernel(scale, *refs), grid=(rows // b...  13 us
  transfers between devices with their start and end apart: 3, of which 0 were waited for; matrix products, arithmetic and copies ran while one was open for 4% of the time, Pallas kernels for 72%

profile of v3, /device:TPU:0, one launch (start us, length us, event | category | flops | bytes accessed | tf_op | source)
XLA Modules:
  0.0 309.6 jit_solution(6477455568784011245)
XLA Ops:
  0.7 0.0 copy-start.15
  0.7 0.8 broadcast_select_fusion.3
  1.5 3.0 collective-permute-start
  4.5 0.7 broadcast_in_dim.76
  5.2 0.7 convert_element_type.20
  5.9 1.3 convert_reduce_fusion
  7.2 1.4 fusion.4
  8.6 0.0 copy-done.15
  8.6 0.3 copy.67
  8.9 0.0 copy-start.8
  8.9 0.0 copy-start.26
  8.9 0.0 copy-start.7
  8.9 1.0 copy-done.8
  9.9 0.9 select_bitcast_fusion.refs_0_
  10.7 0.0 copy-done.26
  10.8 0.1 pad.16.clone
  10.8 0.0 copy-done.7
  10.8 0.3 fusion.6.refs_9_
  11.1 0.1 copy-done.11
  11.2 0.0 copy-start.19
  11.2 0.0 copy-start.20
  11.2 0.0 copy-start.21
  11.3 0.0 copy-start.23
  11.3 0.0 copy-start.24
  11.3 0.3 convolution_convert_fusion.1.refs_3_
  11.6 0.3 copy-done.12
  11.9 0.1 maximum_maximum_fusion.refs_1_
  12.0 0.0 copy-done.25
  12.1 0.8 pad.8.refs_22_
  12.9 0.0 copy-done.22
  12.9 0.0 copy-start.5
  12.9 0.6 broadcast_in_dim.79.refs_2_
  13.5 0.6 broadcast_in_dim.80.refs_3_
  14.1 0.0 copy-done.20
  14.1 0.6 broadcast_in_dim.81.refs_4_
  14.7 0.6 broadcast_in_dim.82.refs_5_
  15.3 0.6 broadcast_in_dim.83.refs_6_
  15.9 0.6 broadcast_in_dim.84.refs_7_
  16.5 0.0 collective-permute-done
  16.5 0.6 pad_add_fusion.refs_1_
  17.1 0.0 collective-permute-start.1
  17.1 0.1 fusion.9
  17.2 0.0 copy-done.13
  17.2 0.3 convolution_convert_fusion.refs_4_.refs_15_
  17.6 0.0 copy-start.4
  17.6 13.0 %shard_map.544 = (bf16[2048,768]{1,0:T(8,128)(2,1)}, f32[1,2048]{1,0:T(1,128)S(1)}, f32[256,2048]{1,0:T(8,128)S(1)}, bf16[256,2048]{1,0:T(8,128)(2,1)S(1)}, bf16[256,768]{1,0:T(8,128)(2,1)S(1)}) custom-call(s32[1,2048]{1,0:T(1,128)S(1)} %reshape_select_fusion.refs_0_.refs_17_, bf16[384,768]{1,0:T(8,128)(2,1)S(1)} %maximum_maximum_fusion.refs_1_, ...), custom_call_target="tpu_custom_call" | custom-call | tf_op jit(solution)/shard_map/pallas_call | solution.py:568
  30.6 0.0 copy-done.5
  30.6 0.0 copy-done
  30.6 0.0 copy-done.4
  30.6 0.0 copy-start.3
  30.6 1.0 copy-done.3
  31.6 0.0 collective-permute-done.1
  31.6 0.1 bitcast_select_fusion.1
  31.7 1.2 copy-done.1
  32.9 0.2 copy-done.2
  33.0 1.1 fusion.7.refs_24_
  34.1 58.9 %shard_map.546 = (bf16[256,1280]{1,0:T(8,128)(2,1)}, bf16[256,1280]{1,0:T(8,128)(2,1)}, bf16[256,1280]{1,0:T(8,128)(2,1)}, bf16[256,1280]{1,0:T(8,128)(2,1)}, bf...) custom-call(bf16[256,1280]{1,0:T(8,128)(2,1)} %refs_6_.1, ...), custom_call_target="tpu_custom_call" | custom-call | tf_op jit(solution)/shard_map/pallas_call | solution.py:681
  93.1 2.1 collective-permute-start.2
  95.1 0.6 broadcast_in_dim.89.refs_10_
  95.7 17.6 %shard_map.547 = (bf16[768,256]{1,0:T(8,128)(2,1)}, bf16[256,256]{1,0:T(8,128)(2,1)}, bf16[256,1280]{1,0:T(8,128)(2,1)}, bf16[768,1280]{1,0:T(8,128)(2,1)}, bf16...) custom-call(bf16[256,768]{1,0:T(8,128)(2,1)} %get-tuple-element.144.refs_0_, ...), custom_call_target="tpu_custom_call" | custom-call | tf_op jit(solution)/shard_map/pallas_call | solution.py:681
  113.4 189.2 %shard_map.548 = (f32[40,1280]{1,0:T(8,128)}, f32[40,1280]{1,0:T(8,128)}, f32[40,1280]{1,0:T(8,128)}, f32[40,1280]{1,0:T(8,128)}, f32[40,256]{1,0:T(8,128)}, /*i...) custom-call(bf16[256,1280]{1,0:T(8,128)(2,1)} %get-tuple-element.125, ...), custom_call_target="tpu_custom_call" | custom-call | tf_op jit(solution)/shard_map/pallas_call | solution.py:463
  302.6 4.3 %shard_map.549 = (f32[64,768]{1,0:T(8,128)}, f32[24,256]{1,0:T(8,128)}, f32[24,1280]{1,0:T(8,128)}, f32[8,1280]{1,0:T(8,128)}, f32[40,256]{1,0:T(8,128)}, /*inde...) custom-call(f32[64,768]{1,0:T(8,128)} %get-tuple-element.164.refs_0_, ...), custom_call_target="tpu_custom_call" | custom-call | tf_op jit(solution)/shard_map/pallas_call | solution.py:511
  307.0 0.0 collective-permute-done.2
  307.1 2.4 broadcast_select_fusion
  (38 shorter events, 0.2 us)
Async XLA Ops:
  0.7 7.9 %copy-start.15 = (bf16[2,1024,262]{1,0,2:T(2,128)(2,1)S(1)}, bf16[2,1024,262]{1,0,2:T(2,128)(2,1)}, u32[]{:S(2)}) copy-start(bf16[2,1024,262]{1,0,2:T(2,128)(2,1)} %param.65) | copy-start | bytes 3219460
  1.5 15.0 %collective-permute-start = (s32[1024]{0:T(1024)S(1)}, s32[1024]{0:T(1024)S(1)}, u32[]{:S(2)}, u32[]{:S(2)}) collective-permute-start(s32[1024]{0:T(1024)S(1)} %bitcast.50), channel_id=1, source_target_pairs={{0,1},{1,0},{2,3},{3,2},{4,5},{5,4},{6,7},{7,6},{8,9},{9,8},{10,11... | collective-permute-start | bytes 12296 | tf_op jit(solution)/shard_map/ppermute | solution.py:935
  8.9 1.0 copy-start.8
  8.9 1.9 copy-start.26
  8.9 1.9 copy-start.7
  9.9 1.3 copy-start.11
  10.8 1.1 copy-start.12
  11.2 1.7 copy-start.10
  11.2 0.8 copy-start.25
  11.2 1.7 copy-start.22
  11.2 1.7 copy-start.18
  11.2 2.3 copy-start.19
  11.2 2.9 copy-start.20
  11.2 3.5 %copy-start.21 = (bf16[1280]{0:T(1024)(128)(2,1)S(1)}, bf16[1280]{0:T(1024)(128)(2,1)}, u32[]{:S(2)}) copy-start(bf16[1280]{0:T(1024)(128)(2,1)} %param.57) | copy-start | bytes 7684
  11.3 4.1 %copy-start.23 = (bf16[768]{0:T(1024)(128)(2,1)S(1)}, bf16[768]{0:T(1024)(128)(2,1)}, u32[]{:S(2)}) copy-start(bf16[768]{0:T(1024)(128)(2,1)} %param.61) | copy-start | bytes 4612
  11.3 4.6 %copy-start.24 = (bf16[768]{0:T(1024)(128)(2,1)S(1)}, bf16[768]{0:T(1024)(128)(2,1)}, u32[]{:S(2)}) copy-start(bf16[768]{0:T(1024)(128)(2,1)} %param.64) | copy-start | bytes 4612
  11.9 5.3 %copy-start.14 = (bf16[256,256]{1,0:T(8,128)(2,1)}, bf16[256,256]{1,0:T(8,128)(2,1)S(1)}, u32[]{:S(2)}) copy-start(bf16[256,256]{1,0:T(8,128)(2,1)S(1)} %convolution_convert_fusion.1.refs_3_) | copy-start | bytes 393220
  11.9 5.3 %copy-start.13 = (bf16[768,256]{1,0:T(8,128)(2,1)S(1)}, bf16[768,256]{1,0:T(8,128)(2,1)}, u32[]{:S(2)}) copy-start(bf16[768,256]{1,0:T(8,128)(2,1)} %refs_4_.1) | copy-start | bytes 1179652
  12.9 17.7 %copy-start.5 = (bf16[1,768]{1,0:T(2,128)(2,1)}, bf16[1,768]{1,0:T(2,128)(2,1)S(1)}, u32[]{:S(2)}) copy-start(bf16[1,768]{1,0:T(2,128)(2,1)S(1)} %broadcast_in_dim.78.refs_3_.refs_18_) | copy-start | bytes 4612
  17.1 14.5 %collective-permute-start.1 = (bf16[262,1024]{1,0:T(8,128)(2,1)}, bf16[262,1024]{1,0:T(8,128)(2,1)S(1)}, u32[]{:S(2)}, u32[]{:S(2)}) collective-permute-start(bf16[262,1024]{1,0:T(8,128)(2,1)} %shard_map.545), channel_id=1, source_target_pairs={{0,1},{1,0},{2,3},{3,2},{4,5},{5,4},{6,7},{7,6},{8,9},{9,8},{10,11... | collective-permute-start | bytes 1609736 | tf_op jit(solution)/shard_map/ppermute | solution.py:935
  17.5 13.0 %copy-start = (bf16[256,768]{1,0:T(8,128)(2,1)}, bf16[256,768]{1,0:T(8,128)(2,1)S(1)}, u32[]{:S(2)}) copy-start(bf16[256,768]{1,0:T(8,128)(2,1)S(1)} %convolution_convert_fusion.refs_4_.refs_15_) | copy-start | bytes 1179652
  17.6 13.0 %copy-start.4 = (s32[1,2048]{1,0:T(1,128)}, s32[1,2048]{1,0:T(1,128)S(1)}, u32[]{:S(2)}) copy-start(s32[1,2048]{1,0:T(1,128)S(1)} %reshape_select_fusion.refs_0_.refs_17_) | copy-start | bytes 24580
  17.6 14.0 %copy-start.9 = (bf16[2,1024,262]{1,2,0:T(8,128)(2,1)S(1)}, bf16[2,1024,262]{1,2,0:T(8,128)(2,1)}, u32[]{:S(2)}) copy-start(bf16[2,1024,262]{1,2,0:T(8,128)(2,1)} %copy-done.8) | copy-start | bytes 3219460
  30.6 1.0 copy-start.3
  31.6 1.3 copy-start.1
  31.6 1.5 copy-start.2
  31.6 1.5 copy-start.6
  34.1 61.0 %copy-start.17 = (bf16[1280]{0:T(1024)(128)(2,1)S(1)}, bf16[1280]{0:T(1024)(128)(2,1)}, u32[]{:S(2)}) copy-start(bf16[1280]{0:T(1024)(128)(2,1)} %param.43) | copy-start | bytes 7684
  93.1 213.9 %collective-permute-start.2 = (bf16[272,1024]{1,0:T(8,128)(2,1)}, bf16[272,1024]{1,0:T(8,128)(2,1)S(1)}, u32[]{:S(2)}, u32[]{:S(2)}) collective-permute-start(bf16[272,1024]{1,0:T(8,128)(2,1)} %get-tuple-element.124), channel_id=1, source_target_pairs={{0,1},{1,0},{2,3},{3,2},{4,5},{5,4},{6,7},{7,6},{8,9},{9,8},{10,11... | collective-permute-start | bytes 1671176 | tf_op jit(solution)/shard_map/ppermute | solution.py:935
  302.6 4.3 %copy-start.16 = (bf16[272,1024]{1,0:T(8,128)(2,1)S(1)}, bf16[272,1024]{1,0:T(8,128)(2,1)}, u32[]{:S(2)}) copy-start(bf16[272,1024]{1,0:T(8,128)(2,1)} %get-tuple-element.123) | copy-start | bytes 1671172

commit v4 on v3

--- a/solution.py
+++ b/solution.py
@@ -551,7 +551,7 @@
 
 def bytes_forward(codes, table, position, gain, qk, scale):
     rows, width = position.shape
-    latents, block = qk.shape[0], 256
+    latents, block = qk.shape[0], 512
 
     def whole(x):
         return pl.BlockSpec(x.shape, lambda i: (0, 0))
@@ -695,7 +695,7 @@
     vd, nb, soft, q, w_key, w_query, latent = arrays[:7]
     rows, width = nb.shape
     latents, features = latent.shape
-    entries, block = -(-arrays[12].shape[0] // 128) * 128, 256
+    entries, block = -(-arrays[12].shape[0] // 128) * 128, 512
     steps = rows // block
 
     def body(small, w, results, extra):

time: 314 us -> 311 us (level)
  transfers between devices with their start and end apart: 3 -> 3, of which waited for: 0 -> 1; matrix products, arithmetic and copies ran while one was open for 4% -> 4% of each run, Pallas kernels for 72% -> 72%
where the time goes in v4:
time: 311 us; the launch traced here: 306 us
  Pallas kernels  280 us (90%)
  other arithmetic  9.8 us (3%)
  local copies, waits for them, and re-layouts  8.46 us (3%)
  starting transfers between devices  4.91 us (2%)
    pallas_call x1, Pallas kernels, reduce_all(): pl.pallas_call(lambda *refs: reduce_kernel(plan, *refs), out_shape=[jax.S...  189 us
    pallas_call x2, Pallas kernels, streamed(): pl.pallas_call(kernel, out_shape=shapes, in_specs=[pl.BlockSpec(memory_sp...  75 us
    pallas_call x1, Pallas kernels, bytes_forward(): pl.pallas_call(lambda *refs: lookup_kernel(scale, *refs), grid=(rows // b...  10.9 us
  transfers between devices with their start and end apart: 3, of which 1 were waited for; matrix products, arithmetic and copies ran while one was open for 4% of the time, Pallas kernels for 72%

profile of v4, /device:TPU:0, one launch (start us, length us, event | category | flops | bytes accessed | tf_op | source)
XLA Modules:
  0.0 306.2 jit_solution(17375337626009474171)
XLA Ops:
  0.7 0.0 copy-start.15
  0.7 0.8 broadcast_select_fusion.3
  1.5 3.0 collective-permute-start
  4.5 0.7 broadcast_in_dim.76
  5.2 0.7 convert_element_type.20
  5.9 1.3 convert_reduce_fusion
  7.2 1.4 fusion.4
  8.6 0.0 copy-done.15
  8.6 0.3 copy.67
  8.9 0.0 copy-start.8
  8.9 0.0 copy-start.26
  8.9 0.0 copy-start.7
  8.9 1.0 copy-done.8
  9.9 0.9 select_bitcast_fusion.refs_0_
  10.7 0.0 copy-done.26
  10.8 0.1 pad.16.clone
  10.8 0.0 copy-done.7
  10.8 0.3 fusion.6.refs_9_
  11.1 0.1 copy-done.11
  11.2 0.0 copy-start.19
  11.2 0.0 copy-start.20
  11.2 0.0 copy-start.21
  11.3 0.0 copy-start.23
  11.3 0.0 copy-start.24
  11.3 0.3 convolution_convert_fusion.1.refs_3_
  11.6 0.3 copy-done.12
  11.9 0.1 maximum_maximum_fusion.refs_1_
  12.0 0.0 copy-done.25
  12.1 0.8 pad.8.refs_22_
  12.9 0.0 copy-done.10
  12.9 0.0 copy-start.5
  12.9 0.6 broadcast_in_dim.79.refs_2_
  13.5 0.0 copy-done.19
  13.5 0.6 broadcast_in_dim.80.refs_3_
  14.1 0.6 broadcast_in_dim.81.refs_4_
  14.7 0.6 broadcast_in_dim.82.refs_5_
  15.3 0.0 copy-done.23
  15.3 0.6 broadcast_in_dim.83.refs_6_
  15.9 0.0 copy-done.24
  15.9 0.6 broadcast_in_dim.84.refs_7_
  16.5 0.0 collective-permute-done
  16.5 0.6 pad_add_fusion.refs_1_
  17.1 0.0 collective-permute-start.1
  17.1 0.1 fusion.9
  17.2 0.0 copy-done.14
  17.2 0.3 convolution_convert_fusion.refs_4_.refs_15_
  17.6 0.0 copy-start.4
  17.6 10.9 %shard_map.544 = (bf16[2048,768]{1,0:T(8,128)(2,1)}, f32[1,2048]{1,0:T(1,128)S(1)}, f32[256,2048]{1,0:T(8,128)S(1)}, bf16[256,2048]{1,0:T(8,128)(2,1)S(1)}, bf16[256,768]{1,0:T(8,128)(2,1)S(1)}) custom-call(s32[1,2048]{1,0:T(1,128)S(1)} %reshape_select_fusion.refs_0_.refs_17_, bf16[384,768]{1,0:T(8,128)(2,1)S(1)} %maximum_maximum_fusion.refs_1_, ...), custom_call_target="tpu_custom_call" | custom-call | tf_op jit(solution)/shard_map/pallas_call | solution.py:568
  28.5 0.0 copy-start.3
  28.5 1.0 copy-done.3
  29.5 1.5 collective-permute-done.1
  31.0 0.1 bitcast_select_fusion.1
  31.1 0.0 copy-done.1
  31.2 0.0 copy-done.2
  31.2 0.0 copy-done.6
  31.2 1.1 fusion.7.refs_24_
  32.3 58.9 %shard_map.546 = (bf16[256,1280]{1,0:T(8,128)(2,1)}, bf16[256,1280]{1,0:T(8,128)(2,1)}, bf16[256,1280]{1,0:T(8,128)(2,1)}, bf16[256,1280]{1,0:T(8,128)(2,1)}, bf...) custom-call(bf16[256,1280]{1,0:T(8,128)(2,1)} %refs_6_.1, ...), custom_call_target="tpu_custom_call" | custom-call | tf_op jit(solution)/shard_map/pallas_call | solution.py:681
  91.2 1.9 collective-permute-start.2
  93.1 0.6 broadcast_in_dim.89.refs_10_
  93.7 16.1 %shard_map.547 = (bf16[768,256]{1,0:T(8,128)(2,1)}, bf16[256,256]{1,0:T(8,128)(2,1)}, bf16[256,1280]{1,0:T(8,128)(2,1)}, bf16[768,1280]{1,0:T(8,128)(2,1)}, bf16...) custom-call(bf16[256,768]{1,0:T(8,128)(2,1)} %get-tuple-element.144.refs_0_, ...), custom_call_target="tpu_custom_call" | custom-call | tf_op jit(solution)/shard_map/pallas_call | solution.py:681
  109.8 189.4 %shard_map.548 = (f32[40,1280]{1,0:T(8,128)}, f32[40,1280]{1,0:T(8,128)}, f32[40,1280]{1,0:T(8,128)}, f32[40,1280]{1,0:T(8,128)}, f32[40,256]{1,0:T(8,128)}, /*i...) custom-call(bf16[256,1280]{1,0:T(8,128)(2,1)} %get-tuple-element.125, ...), custom_call_target="tpu_custom_call" | custom-call | tf_op jit(solution)/shard_map/pallas_call | solution.py:463
  299.2 4.3 %shard_map.549 = (f32[64,768]{1,0:T(8,128)}, f32[24,256]{1,0:T(8,128)}, f32[24,1280]{1,0:T(8,128)}, f32[8,1280]{1,0:T(8,128)}, f32[40,256]{1,0:T(8,128)}, /*inde...) custom-call(f32[64,768]{1,0:T(8,128)} %get-tuple-element.164.refs_0_, ...), custom_call_target="tpu_custom_call" | custom-call | tf_op jit(solution)/shard_map/pallas_call | solution.py:511
  303.6 0.0 collective-permute-done.2
  303.6 2.4 broadcast_select_fusion
  (38 shorter events, 0.2 us)
Async XLA Ops:
  0.7 7.9 %copy-start.15 = (bf16[2,1024,262]{1,0,2:T(2,128)(2,1)S(1)}, bf16[2,1024,262]{1,0,2:T(2,128)(2,1)}, u32[]{:S(2)}) copy-start(bf16[2,1024,262]{1,0,2:T(2,128)(2,1)} %param.65) | copy-start | bytes 3219460
  1.5 15.0 %collective-permute-start = (s32[1024]{0:T(1024)S(1)}, s32[1024]{0:T(1024)S(1)}, u32[]{:S(2)}, u32[]{:S(2)}) collective-permute-start(s32[1024]{0:T(1024)S(1)} %bitcast.50), channel_id=1, source_target_pairs={{0,1},{1,0},{2,3},{3,2},{4,5},{5,4},{6,7},{7,6},{8,9},{9,8},{10,11... | collective-permute-start | bytes 12296 | tf_op jit(solution)/shard_map/ppermute | solution.py:935
  8.9 1.0 copy-start.8
  8.9 1.9 copy-start.26
  8.9 1.9 copy-start.7
  9.9 1.3 copy-start.11
  10.8 1.1 copy-start.12
  11.2 1.7 copy-start.10
  11.2 0.8 copy-start.25
  11.2 1.7 copy-start.22
  11.2 1.7 copy-start.18
  11.2 2.3 copy-start.19
  11.2 2.9 copy-start.20
  11.2 3.5 %copy-start.21 = (bf16[1280]{0:T(1024)(128)(2,1)S(1)}, bf16[1280]{0:T(1024)(128)(2,1)}, u32[]{:S(2)}) copy-start(bf16[1280]{0:T(1024)(128)(2,1)} %param.57) | copy-start | bytes 7684
  11.3 4.1 %copy-start.23 = (bf16[768]{0:T(1024)(128)(2,1)S(1)}, bf16[768]{0:T(1024)(128)(2,1)}, u32[]{:S(2)}) copy-start(bf16[768]{0:T(1024)(128)(2,1)} %param.61) | copy-start | bytes 4612
  11.3 4.6 %copy-start.24 = (bf16[768]{0:T(1024)(128)(2,1)S(1)}, bf16[768]{0:T(1024)(128)(2,1)}, u32[]{:S(2)}) copy-start(bf16[768]{0:T(1024)(128)(2,1)} %param.64) | copy-start | bytes 4612
  11.9 5.3 %copy-start.14 = (bf16[256,256]{1,0:T(8,128)(2,1)}, bf16[256,256]{1,0:T(8,128)(2,1)S(1)}, u32[]{:S(2)}) copy-start(bf16[256,256]{1,0:T(8,128)(2,1)S(1)} %convolution_convert_fusion.1.refs_3_) | copy-start | bytes 393220
  11.9 5.3 %copy-start.13 = (bf16[768,256]{1,0:T(8,128)(2,1)S(1)}, bf16[768,256]{1,0:T(8,128)(2,1)}, u32[]{:S(2)}) copy-start(bf16[768,256]{1,0:T(8,128)(2,1)} %refs_4_.1) | copy-start | bytes 1179652
  12.9 15.6 %copy-start.5 = (bf16[1,768]{1,0:T(2,128)(2,1)}, bf16[1,768]{1,0:T(2,128)(2,1)S(1)}, u32[]{:S(2)}) copy-start(bf16[1,768]{1,0:T(2,128)(2,1)S(1)} %broadcast_in_dim.78.refs_3_.refs_18_) | copy-start | bytes 4612
  17.1 13.9 %collective-permute-start.1 = (bf16[262,1024]{1,0:T(8,128)(2,1)}, bf16[262,1024]{1,0:T(8,128)(2,1)S(1)}, u32[]{:S(2)}, u32[]{:S(2)}) collective-permute-start(bf16[262,1024]{1,0:T(8,128)(2,1)} %shard_map.545), channel_id=1, source_target_pairs={{0,1},{1,0},{2,3},{3,2},{4,5},{5,4},{6,7},{7,6},{8,9},{9,8},{10,11... | collective-permute-start | bytes 1609736 | tf_op jit(solution)/shard_map/ppermute | solution.py:935
  17.5 11.0 %copy-start = (bf16[256,768]{1,0:T(8,128)(2,1)}, bf16[256,768]{1,0:T(8,128)(2,1)S(1)}, u32[]{:S(2)}) copy-start(bf16[256,768]{1,0:T(8,128)(2,1)S(1)} %convolution_convert_fusion.refs_4_.refs_15_) | copy-start | bytes 1179652
  17.6 10.9 %copy-start.4 = (s32[1,2048]{1,0:T(1,128)}, s32[1,2048]{1,0:T(1,128)S(1)}, u32[]{:S(2)}) copy-start(s32[1,2048]{1,0:T(1,128)S(1)} %reshape_select_fusion.refs_0_.refs_17_) | copy-start | bytes 24580
  17.6 13.5 %copy-start.9 = (bf16[2,1024,262]{1,2,0:T(8,128)(2,1)S(1)}, bf16[2,1024,262]{1,2,0:T(8,128)(2,1)}, u32[]{:S(2)}) copy-start(bf16[2,1024,262]{1,2,0:T(8,128)(2,1)} %copy-done.8) | copy-start | bytes 3219460
  28.5 1.0 copy-start.3
  29.5 1.6 copy-start.1
  29.5 1.7 copy-start.2
  29.5 1.7 copy-start.6
  32.3 60.8 %copy-start.17 = (bf16[1280]{0:T(1024)(128)(2,1)S(1)}, bf16[1280]{0:T(1024)(128)(2,1)}, u32[]{:S(2)}) copy-start(bf16[1280]{0:T(1024)(128)(2,1)} %param.43) | copy-start | bytes 7684
  91.2 212.4 %collective-permute-start.2 = (bf16[272,1024]{1,0:T(8,128)(2,1)}, bf16[272,1024]{1,0:T(8,128)(2,1)S(1)}, u32[]{:S(2)}, u32[]{:S(2)}) collective-permute-start(bf16[272,1024]{1,0:T(8,128)(2,1)} %get-tuple-element.124), channel_id=1, source_target_pairs={{0,1},{1,0},{2,3},{3,2},{4,5},{5,4},{6,7},{7,6},{8,9},{9,8},{10,11... | collective-permute-start | bytes 1671176 | tf_op jit(solution)/shard_map/ppermute | solution.py:935
  299.2 4.3 %copy-start.16 = (bf16[272,1024]{1,0:T(8,128)(2,1)S(1)}, bf16[272,1024]{1,0:T(8,128)(2,1)}, u32[]{:S(2)}) copy-start(bf16[272,1024]{1,0:T(8,128)(2,1)} %get-tuple-element.123) | copy-start | bytes 1671172
